TPU v7x, 32 devices: a whole 2x2x4 slice. The times are simulated.
32 devices in a mesh: off: 2 (over core), win: 16 (over z, y, x).
Axes of the slice: x: 2, y: 2, z: 4, core: 2. Of those that a mesh axis runs over, the one named last changes fastest.
Arguments:
- kernels: float32 [2, 16, 16, 64, 128], P('off', 'win'), may hold values from -6 to 6
- blocks: int32 [2, 16, 16, 128], P('off', 'win'), may hold values from 0 to 2047
- counts: int32 [2, 16, 16], P('off', 'win'), may hold values from 1 to 128, as said below
- ray_of: int32 [2, 16, 16, 128], P('off', 'win'), may hold values from 0 to 511
- slopes: float32 [2, 16, 512], P('off', 'win'), may hold values from -6 to 6
Outputs:
- update: float32 [64, 32768], P(None, 'win')
- data_vector: float32 [2, 16, 512], P('off', 'win')
Inputs may be any that keep to these rules, and one draw needn't show every extreme that they name: `counts`: some event windows, drawn from the seed (each with chance one in four), carry more segments each than the rest; one owner, drawn from the seed, receives 128 live slots from every window of every offset class.
All inputs are finite; a program needn't handle non-finite values.
Results may differ from a plain program's by a relative error of at most 0.0003.
Values sent between devices are 32-bit elements; how exact they have to be, the bound alone decides.
A program may use at most 64 MiB of HBM per device.

v0:
```python
import jax
import jax.numpy as jnp
from jax import lax
from jax.sharding import PartitionSpec as P

BLK_DEV = 2048
ITERS = 3


def body(kernels, blocks, counts, ray_of, slopes):
    windows = lax.axis_size("win")
    cells = kernels.shape[3]
    slots = kernels.shape[4]
    ray_count = slopes.shape[2]
    live = (
        lax.broadcasted_iota(jnp.int32, (1, 1, windows, 1, slots), 4) < counts[:, :, :, None, None]
    )
    masked = jnp.where(live, kernels, jnp.zeros_like(kernels))
    ray_flat = ray_of.reshape(-1)

    def data_norm(vector):
        return lax.psum(jnp.sum(vector * vector), ("off", "win"))

    def model_norm(vector):
        return lax.psum(jnp.sum(vector * vector), "win")

    def accumulate(contrib, owned_ids):
        flat = jnp.moveaxis(contrib, 3, 0).reshape(cells, -1)
        local = jnp.zeros((cells, BLK_DEV), jnp.float32).at[:, owned_ids.reshape(-1)].add(flat)
        return lax.psum(local, "off")

    def residual_weights(data):
        return data.reshape(-1)[ray_of]

    held, held_ids = (
        lax.all_to_all(masked, "win", split_axis=2, concat_axis=1, tiled=True),
        lax.all_to_all(blocks, "win", split_axis=2, concat_axis=1, tiled=True),
    )

    def adjoint(data):
        arrived = lax.all_to_all(
            residual_weights(data), "win", split_axis=2, concat_axis=1, tiled=True
        )
        return accumulate(held * arrived[:, :, :, None, :], held_ids)

    beta = jnp.sqrt(data_norm(slopes))
    data_vector = slopes / beta
    model_vec = adjoint(data_vector)
    alpha = jnp.sqrt(model_norm(model_vec))
    model_vec = model_vec / alpha
    search = model_vec
    phibar = beta
    rhobar = alpha
    update = jnp.zeros((cells, BLK_DEV), jnp.float32)
    for step in range(ITERS):
        fetched = jnp.moveaxis(model_vec[:, held_ids], 0, 3)
        forward_values = jnp.sum(held * fetched, axis=3)
        returned = lax.all_to_all(forward_values, "win", split_axis=1, concat_axis=2, tiled=True)
        summed = jax.ops.segment_sum(returned.reshape(-1), ray_flat, num_segments=ray_count)
        data_vector = summed.reshape(1, 1, ray_count) - alpha * data_vector
        beta = jnp.sqrt(data_norm(data_vector))
        data_vector = data_vector / beta
        model_vec = adjoint(data_vector) - beta * model_vec
        alpha = jnp.sqrt(model_norm(model_vec))
        model_vec = model_vec / alpha
        rho = jnp.sqrt(rhobar * rhobar + beta * beta)
        cosine = rhobar / rho
        sine = beta / rho
        theta = sine * alpha
        rhobar = -cosine * alpha
        phi = cosine * phibar
        phibar = sine * phibar
        update = update + phi / rho * search
        search = model_vec - theta / rho * search
    return (update, data_vector)


def solution(mesh):
    in_specs = (
        P("off", "win", None, None, None),
        P("off", "win", None, None),
        P("off", "win", None),
        P("off", "win", None, None),
        P("off", "win", None),
    )
    out_specs = (P(None, "win"), P("off", "win", None))
    return jax.shard_map(body, mesh=mesh, in_specs=in_specs, out_specs=out_specs, check_vma=False)
```

profile of v0, /device:TPU:0, one launch (start us, length us, event | category | flops | bytes accessed | tf_op | source)
XLA Modules:
  0.0 631.4 jit_solution(17009253015936179770)
XLA Ops:
  7.2 1.3 multiply_reduce_fusion.6
  8.5 42.2 %psum.70 = f32[]{:T(128)} all-reduce(f32[]{:T(128)} %multiply_reduce_fusion.6), channel_id=1, replica_groups=mesh['off'=2,'win'=16] {'off','win'}, use_global_device_ids=true, to_apply=%region_1.2 | all-reduce | flops 1 | bytes 8 | tf_op jit(solution)/shard_map/psum | solution.py:22
  52.1 22.0 %gather_fusion = f32[2048]{0:T(1024)} fusion(f32[512]{0:T(512)S(1)} %bitcast.110, s32[2048]{0:T(1024)S(1)} %fusion.13), kind=kCustom, calls=%fused_computation | custom fusion | bytes 24576 | tf_op jit(solution)/shard_map/gather | solution.py:33
  74.1 5.6 all-to-all-start.2
  80.5 6.5 %all-to-all-done.2 = f32[1,1,16,128]{3,1,0,2:T(1,128)S(1)} async-done(((f32[1,1,16,128]{3,1,0,2:T(1,128)}), f32[1,1,16,128]{3,1,0,2:T(1,128)S(1)}, u32[]{:S(2)}, u32[]{:S(2)}) %all-to-all-start.2) | async-done | bytes 8224 | tf_op jit(solution)/shard_map/all_to_all | solution.py:41
  86.9 3.5 all-to-all-start
  91.3 6.3 %all-to-all-done = s32[1,1,16,128]{3,1,0,2:T(1,128)S(1)} async-done(((s32[1,1,16,128]{3,1,0,2:T(1,128)}), s32[1,1,16,128]{3,1,0,2:T(1,128)S(1)}, u32[]{:S(2)}, u32[]{:S(2)}) %all-to-all-start) | async-done | bytes 8224 | tf_op jit(solution)/shard_map/all_to_all | solution.py:37
  97.6 3.6 all-to-all-start.1
  101.2 11.9 %all-to-all-done.1 = f32[1,1,16,64,128]{4,3,1,0,2:T(8,128)S(1)} async-done(((f32[1,1,16,64,128]{4,3,1,0,2:T(8,128)}), f32[1,1,16,64,128]{4,3,1,0,2:T(8,128)S(1)}, u32[]{:S(2)}, u32[]{:S(2)}) %all-to-all-start.1) | async-done | bytes 524320 | tf_op jit(solution)/shard_map/all_to_all | solution.py:36
  114.0 12.5 %scatter_custom_fusion = f32[64,2048]{0,1:T(8,128)} fusion(s32[2048]{0:T(1024)S(1)} %bitcast.137, f32[2048,64]{1,0:T(8,128)S(1)} %copy.24, f32[]{:T(128)} %constant.4.clone.1), kind=kCustom, calls=%fused_computation.41 | custom fusion | flops 131072 | bytes 524292 | tf_op jit(solution)/shard_map/scatter-add | solution.py:29
  126.6 17.9 %all-reduce.4.cloned.1.call-done = f32[64,2048]{0,1:T(8,128)} async-done(((f32[64,2048]{0,1:T(8,128)}), f32[64,2048]{0,1:T(8,128)}) %all-reduce.4.cloned.1.call-update) | async-done | bytes 524304 | tf_op jit(solution)/shard_map/psum | solution.py:30
  144.5 2.2 multiply_reduce_fusion.2
  146.7 42.6 %psum.72 = f32[]{:T(128)} all-reduce(f32[]{:T(128)} %multiply_reduce_fusion.2), channel_id=1, replica_groups=mesh['off'=2,'win'=16] {'win'}, use_global_device_ids=true, to_apply=%region_5.6 | all-reduce | flops 1 | bytes 8 | tf_op jit(solution)/shard_map/psum | solution.py:25
  190.1 7.6 %gather_fusion.1 = f32[2048,64]{1,0:T(8,128)} fusion(f32[64,2048]{0,1:T(8,128)S(1)} %broadcast_divide_fusion.2, s32[2048]{0:T(1024)S(1)} %fusion.15), kind=kCustom, calls=%fused_computation.1 | custom fusion | bytes 1056768 | tf_op jit(solution)/shard_map/gather | solution.py:56
  197.7 1.5 copy.25
  199.3 9.9 %all_to_all.38 = f32[1,16,1,128]{3,2,0,1:T(1,128)S(1)} all-to-all(f32[1,16,1,128]{3,2,0,1:T(1,128)S(1)} %bitcast.122), channel_id=1, replica_groups=mesh['off'=2,'win'=16] {'win'}, dimensions={1} | all-to-all | bytes 16384 | tf_op jit(solution)/shard_map/all_to_all | solution.py:58
  209.2 14.8 %scatter_custom_fusion.1 = f32[512]{0:T(512)S(1)} fusion(s32[2048]{0:T(1024)} %bitcast.134, f32[2048]{0:T(1024)S(1)} %bitcast.141, f32[]{:T(128)} %constant.4.clone.1), kind=kCustom, calls=%fused_computation.65 | custom fusion | flops 2048 | bytes 2560 | tf_op jit(solution)/shard_map/scatter-add | solution.py:59
  224.6 38.5 %psum.73 = f32[]{:T(128)} all-reduce(f32[]{:T(128)} %multiply_reduce_fusion.5), channel_id=1, replica_groups=mesh['off'=2,'win'=16] {'off','win'}, use_global_device_ids=true, to_apply=%region_9.10 | all-reduce | flops 1 | bytes 8 | tf_op jit(solution)/shard_map/psum | solution.py:22
  263.8 13.2 %gather_fusion.2 = f32[2048]{0:T(1024)S(1)} fusion(f32[512]{0:T(512)S(1)} %bitcast.109, s32[2048]{0:T(1024)S(1)} %fusion.13), kind=kCustom, calls=%fused_computation.2 | custom fusion | bytes 24576 | tf_op jit(solution)/shard_map/gather | solution.py:33
  277.0 12.0 %all_to_all.39 = f32[1,1,16,128]{3,1,0,2:T(1,128)S(1)} all-to-all(f32[1,1,16,128]{3,1,0,2:T(1,128)S(1)} %bitcast.127), channel_id=1, replica_groups=mesh['off'=2,'win'=16] {'win'}, dimensions={2} | all-to-all | bytes 16384 | tf_op jit(solution)/shard_map/all_to_all | solution.py:41
  289.5 1.4 copy.27
  290.9 12.8 %scatter_custom_fusion.2 = f32[64,2048]{0,1:T(8,128)} fusion(s32[2048]{0:T(1024)S(1)} %bitcast.138, f32[2048,64]{1,0:T(8,128)} %copy.27, f32[]{:T(128)} %constant.4.clone.1), kind=kCustom, calls=%fused_computation.39 | custom fusion | flops 131072 | bytes 524800 | tf_op jit(solution)/shard_map/scatter-add | solution.py:29
  303.8 16.1 %all-reduce.6.cloned.1.call-done = f32[64,2048]{0,1:T(8,128)} async-done(((f32[64,2048]{0,1:T(8,128)}), f32[64,2048]{0,1:T(8,128)}) %all-reduce.6.cloned.1.call-update) | async-done | bytes 524304 | tf_op jit(solution)/shard_map/psum | solution.py:30
  319.8 2.1 multiply_reduce_fusion.1
  322.0 42.8 %psum.75 = f32[]{:T(128)} all-reduce(f32[]{:T(128)} %multiply_reduce_fusion.1), channel_id=1, replica_groups=mesh['off'=2,'win'=16] {'win'}, use_global_device_ids=true, to_apply=%region_13.14 | all-reduce | flops 1 | bytes 8 | tf_op jit(solution)/shard_map/psum | solution.py:25
  365.4 1.4 broadcast_divide_fusion.1
  366.8 7.6 %gather_fusion.3 = f32[2048,64]{1,0:T(8,128)} fusion(f32[64,2048]{0,1:T(8,128)S(1)} %broadcast_divide_fusion.1, s32[2048]{0:T(1024)S(1)} %fusion.15), kind=kCustom, calls=%fused_computation.3 | custom fusion | bytes 1056768 | tf_op jit(solution)/shard_map/gather | solution.py:56
  374.4 1.5 copy.28
  376.0 9.9 %all_to_all.80 = f32[1,16,1,128]{3,2,0,1:T(1,128)S(1)} all-to-all(f32[1,16,1,128]{3,2,0,1:T(1,128)S(1)} %bitcast.124), channel_id=1, replica_groups=mesh['off'=2,'win'=16] {'win'}, dimensions={1} | all-to-all | bytes 16384 | tf_op jit(solution)/shard_map/all_to_all | solution.py:58
  385.9 14.8 %scatter_custom_fusion.3 = f32[512]{0:T(512)S(1)} fusion(s32[2048]{0:T(1024)} %bitcast.135, f32[2048]{0:T(1024)S(1)} %bitcast.142, f32[]{:T(128)} %constant.4.clone.1), kind=kCustom, calls=%fused_computation.63 | custom fusion | flops 2048 | bytes 2560 | tf_op jit(solution)/shard_map/scatter-add | solution.py:59
  401.3 38.5 %psum.76 = f32[]{:T(128)} all-reduce(f32[]{:T(128)} %multiply_reduce_fusion.4), channel_id=1, replica_groups=mesh['off'=2,'win'=16] {'off','win'}, use_global_device_ids=true, to_apply=%region_17.18 | all-reduce | flops 1 | bytes 8 | tf_op jit(solution)/shard_map/psum | solution.py:22
  440.4 13.2 %gather_fusion.4 = f32[2048]{0:T(1024)S(1)} fusion(f32[512]{0:T(512)S(1)} %bitcast.108, s32[2048]{0:T(1024)S(1)} %fusion.13), kind=kCustom, calls=%fused_computation.4 | custom fusion | bytes 24576 | tf_op jit(solution)/shard_map/gather | solution.py:33
  453.7 12.0 %all_to_all.81 = f32[1,1,16,128]{3,1,0,2:T(1,128)S(1)} all-to-all(f32[1,1,16,128]{3,1,0,2:T(1,128)S(1)} %bitcast.126), channel_id=1, replica_groups=mesh['off'=2,'win'=16] {'win'}, dimensions={2} | all-to-all | bytes 16384 | tf_op jit(solution)/shard_map/all_to_all | solution.py:41
  466.2 1.4 copy.30
  467.5 12.8 %scatter_custom_fusion.4 = f32[64,2048]{0,1:T(8,128)} fusion(s32[2048]{0:T(1024)S(1)} %bitcast.139, f32[2048,64]{1,0:T(8,128)} %copy.30, f32[]{:T(128)} %constant.4.clone.1), kind=kCustom, calls=%fused_computation.37 | custom fusion | flops 131072 | bytes 524800 | tf_op jit(solution)/shard_map/scatter-add | solution.py:29
  480.4 16.1 %all-reduce.8.cloned.1.call-done = f32[64,2048]{0,1:T(8,128)} async-done(((f32[64,2048]{0,1:T(8,128)}), f32[64,2048]{0,1:T(8,128)}) %all-reduce.8.cloned.1.call-update) | async-done | bytes 524304 | tf_op jit(solution)/shard_map/psum | solution.py:30
  496.5 2.1 multiply_reduce_fusion
  498.6 42.6 %psum.78 = f32[]{:T(128)} all-reduce(f32[]{:T(128)} %multiply_reduce_fusion), channel_id=1, replica_groups=mesh['off'=2,'win'=16] {'win'}, use_global_device_ids=true, to_apply=%region_21.22 | all-reduce | flops 1 | bytes 8 | tf_op jit(solution)/shard_map/psum | solution.py:25
  541.9 1.3 broadcast_divide_fusion
  543.2 7.6 %gather_fusion.5 = f32[2048,64]{1,0:T(8,128)} fusion(f32[64,2048]{0,1:T(8,128)S(1)} %broadcast_divide_fusion, s32[2048]{0:T(1024)S(1)} %fusion.15), kind=kCustom, calls=%fused_computation.5 | custom fusion | bytes 1056768 | tf_op jit(solution)/shard_map/gather | solution.py:56
  550.8 2.3 copy.31
  553.2 1.9 fusion
  555.0 3.5 all-to-all-start.7
  558.9 6.8 %all-to-all-done.7 = f32[1,16,1,128]{3,2,0,1:T(1,128)S(1)} async-done(((f32[1,16,1,128]{3,2,0,1:T(1,128)}), f32[1,16,1,128]{3,2,0,1:T(1,128)S(1)}, u32[]{:S(2)}, u32[]{:S(2)}) %all-to-all-start.7) | async-done | bytes 8224 | tf_op jit(solution)/shard_map/all_to_all | solution.py:58
  565.8 14.8 %scatter_custom_fusion.5 = f32[512]{0:T(512)S(1)} fusion(s32[2048]{0:T(1024)} %bitcast.136, f32[2048]{0:T(1024)S(1)} %bitcast.140, f32[]{:T(128)} %constant.4.clone.1), kind=kCustom, calls=%fused_computation.61 | custom fusion | flops 2048 | bytes 2560 | tf_op jit(solution)/shard_map/scatter-add | solution.py:59
  581.2 38.5 %psum.79 = f32[]{:T(128)} all-reduce(f32[]{:T(128)} %multiply_reduce_fusion.3), channel_id=1, replica_groups=mesh['off'=2,'win'=16] {'off','win'}, use_global_device_ids=true, to_apply=%region_25.26 | all-reduce | flops 1 | bytes 8 | tf_op jit(solution)/shard_map/psum | solution.py:22
  621.2 1.4 multiply_add_fusion
  622.6 2.3 copy.32
  (41 shorter events, 7.0 us)
Async XLA Ops:
  8.5 42.9 %copy-start.3 = (f32[1,1,512]{2,1,0:T(1,128)S(1)}, f32[1,1,512]{2,1,0:T(1,128)}, u32[]{:S(2)}) copy-start(f32[1,1,512]{2,1,0:T(1,128)} %param.9) | copy-start | bytes 6148
  52.1 38.3 %copy-start.2 = (f32[1,1,16,64,128]{4,3,2,1,0:T(8,128)S(1)}, f32[1,1,16,64,128]{4,3,2,1,0:T(8,128)}, u32[]{:S(2)}) copy-start(f32[1,1,16,64,128]{4,3,2,1,0:T(8,128)} %param.5) | copy-start | bytes 1572868
  74.1 12.8 %all-to-all-start.2 = ((f32[1,1,16,128]{3,1,0,2:T(1,128)}), f32[1,1,16,128]{3,1,0,2:T(1,128)S(1)}, u32[]{:S(2)}, u32[]{:S(2)}) async-start(f32[1,1,16,128]{3,1,0,2:T(1,128)} %bitcast.8), calls=%async_computation.2 | async-start | bytes 16384 | tf_op jit(solution)/shard_map/all_to_all | solution.py:41
  79.7 0.7 copy-start.4
  86.9 10.6 %all-to-all-start = ((s32[1,1,16,128]{3,1,0,2:T(1,128)}), s32[1,1,16,128]{3,1,0,2:T(1,128)S(1)}, u32[]{:S(2)}, u32[]{:S(2)}) async-start(s32[1,1,16,128]{3,1,0,2:T(1,128)} %bitcast), calls=%async_computation | async-start | bytes 16384 | tf_op jit(solution)/shard_map/all_to_all | solution.py:37
  97.6 15.6 %all-to-all-start.1 = ((f32[1,1,16,64,128]{4,3,1,0,2:T(8,128)}), f32[1,1,16,64,128]{4,3,1,0,2:T(8,128)S(1)}, u32[]{:S(2)}, u32[]{:S(2)}) async-start(f32[1,1,16,64,128]{4,3,1,0,2:T(8,128)} %bitcast_select_fusion), calls=%async_computation.1 | async-start | bytes 1048576 | tf_op jit(solution)/shard_map/all_to_all | solution.py:36
  101.2 43.4 %all-reduce.4.cloned.1.call-start = ((), (), s32[]{:S(2)}) async-start(), calls=%async_computation.8 | async-start | bytes 2097152 | tf_op jit(solution)/shard_map/psum | solution.py:30
  113.1 352.5 %copy-start.1 = (f32[1,1,16,64,128]{4,3,1,0,2:T(8,128)}, f32[1,1,16,64,128]{4,3,1,0,2:T(8,128)S(1)}, u32[]{:S(2)}) copy-start(f32[1,1,16,64,128]{4,3,1,0,2:T(8,128)S(1)} %all-to-all-done.1) | copy-start | bytes 1572868
  126.5 193.3 %all-reduce.6.cloned.1.call-start = ((), (), s32[]{:S(2)}) async-start(), calls=%async_computation.9 | async-start | bytes 2097152 | tf_op jit(solution)/shard_map/psum | solution.py:30
  144.5 45.5 %copy-start = (f32[64,2048]{0,1:T(8,128)S(1)}, f32[64,2048]{0,1:T(8,128)}, u32[]{:S(2)}) copy-start(f32[64,2048]{0,1:T(8,128)} %all-reduce.4.cloned.1.call-done) | copy-start | bytes 1572868
  303.7 192.8 %all-reduce.8.cloned.1.call-start = ((), (), s32[]{:S(2)}) async-start(), calls=%async_computation.10 | async-start | bytes 2097152 | tf_op jit(solution)/shard_map/psum | solution.py:30
  555.0 10.7 %all-to-all-start.7 = ((f32[1,16,1,128]{3,2,0,1:T(1,128)}), f32[1,16,1,128]{3,2,0,1:T(1,128)S(1)}, u32[]{:S(2)}, u32[]{:S(2)}) async-start(f32[1,16,1,128]{3,2,0,1:T(1,128)} %bitcast.43), calls=%async_computation.7 | async-start | bytes 16384 | tf_op jit(solution)/shard_map/all_to_all | solution.py:58
Sparse Core Ops, SparseCore 0:
  126.7 17.8 all-reduce.3
  303.8 15.9 all-reduce.5
  480.5 15.9 all-reduce.7
where the time goes:
time: 633 us; the launch traced here: 631 us
  blocking collectives  329 us (52%)
  other arithmetic  101 us (16%)
  local copies, waits for them, and re-layouts  84.1 us (13%)
  waiting for transfers between devices  81.7 us (13%)
  between operations  19.4 us (3%)
  starting transfers between devices  16.3 us (3%)
    psum x4, blocking collectives, data_norm(): return lax.psum(jnp.sum(vector * vector), ('off', 'win'))  158 us
    psum x3, blocking collectives, model_norm(): return lax.psum(jnp.sum(vector * vector), 'win')  128 us
    psum x3, waiting for transfers between devices, accumulate(): return lax.psum(local, 'off')  50.2 us
    gather x3, local copies, waits for them, and re-layouts, residual_weights(): return data.reshape(-1)[ray_of]  48.5 us
    scatter-add x3, other arithmetic, body(): jax.ops.segment_sum(returned.reshape(-1), ray_flat, num_segments=ray_count)  44.4 us
    scatter-add x3, other arithmetic, accumulate(): jnp.zeros((cells, BLK_DEV), jnp.float32).at[:, owned_ids.reshape(-1)]  38.2 us
    gather x6, local copies, waits for them, and re-layouts, body(): fetched = jnp.moveaxis(model_vec[:, held_ids], 0, 3)  28.2 us
    all_to_all x2, blocking collectives, adjoint(): lax.all_to_all(residual_weights(data), 'win', split_axis=2, concat_axis=1...  23.9 us
  transfers between devices with their start and end apart: 7, of which 7 were waited for; matrix products, arithmetic and copies ran while one was open for 0% of the time, Pallas kernels for 0%

commit v1 on v0

v1 whole, which is shorter than its diff:
```python
import functools

import jax
import jax.numpy as jnp
from jax import lax
from jax.experimental import pallas as pl
from jax.experimental.pallas import tpu as pltpu
from jax.sharding import PartitionSpec as P

BLK_DEV = 2048
ITERS = 3
LOW = 256
HIGH = BLK_DEV // LOW
GROUP = 4
LANES = 128

F32 = jnp.float32
BF16 = jnp.bfloat16
MESH = pl.DeviceIdType.MESH


def split2(x):
    top = x.astype(BF16)
    rest = (x - top.astype(F32)).astype(BF16)
    return top, rest


def rows_of(x):
    a = x.astype(BF16).astype(F32)
    b = (x - a).astype(BF16).astype(F32)
    c = x - a - b
    shape = (16, x.shape[1])
    i = lax.broadcasted_iota(jnp.int32, shape, 0)
    wide = lambda y: jnp.broadcast_to(y, shape)
    zero = jnp.zeros(shape, F32)
    return jnp.where(i == 0, wide(a), jnp.where(i == 1, wide(b), jnp.where(i == 2, wide(c), zero))).astype(BF16)


def fold(x):
    return sum(x[:, i : i + LANES] for i in range(0, x.shape[1], LANES))


def kernel(
    offs, wins, kern_ref, block_ref, count_ref, ray_ref, slope_ref,
    out_ref, data_ref,
    rays1h, low1h, held, first_send, first_recv, w_send, w_recv, f_send, f_recv, s_send, s_recv,
    acc, vec, raw, upd, srch,
    send_sem, recv_sem, kern_send, kern_recv, pair_send, pair_recv,
):
    total = offs * wins
    cells = kern_ref.shape[1]
    part = cells // offs
    slots = kern_ref.shape[2]
    rays = slope_ref.shape[1]
    groups = total // GROUP
    width = GROUP * slots
    my_off = lax.axis_index("off")
    my_win = lax.axis_index("win")
    me = my_win * offs + my_off

    def place(index):
        return (lax.rem(index, offs), index // offs)

    def to_of(k):
        return lax.rem(me + k, total)

    def from_of(k):
        return lax.rem(me + total - k, total)

    barrier = pltpu.get_barrier_semaphore()

    @pl.loop(1, total)
    def _(k):
        pl.semaphore_signal(barrier, inc=1, device_id=place(to_of(k)), device_id_type=MESH)

    ray_iota = lax.broadcasted_iota(jnp.int32, (rays, slots), 0)
    lane = lax.broadcasted_iota(jnp.int32, (1, slots), 1)
    for p in range(wins):
        ids = jnp.where(lane < count_ref[p], ray_ref[p : p + 1, :], -1)
        rays1h[:, p * slots : (p + 1) * slots] = jnp.where(ray_iota == ids, 1.0, 0.0).astype(BF16)

    def take(data):
        return jnp.sum(jnp.dot(rows_of(data), rays1h[...], preferred_element_type=F32), axis=0, keepdims=True)

    def gather_rays(values):
        got = lax.dot_general(rows_of(values), rays1h[...], (((1,), (1,)), ((), ())), preferred_element_type=F32)
        return jnp.sum(got, axis=0, keepdims=True)

    def total_of(partials):
        return jnp.sum(jnp.sum(partials, axis=0), axis=1, keepdims=True)

    data = slope_ref[...]
    weights = take(data)
    partial = fold(data * data)
    for p in range(wins):
        ids = block_ref[p : p + 1, :]
        high = ids // LOW
        first_send[p, :, 0:slots] = weights[:, p * slots : (p + 1) * slots]
        first_send[p, :, slots : 2 * slots] = partial
        first_send[p, :, 2 * slots : 3 * slots] = (ids - high * LOW).astype(F32)
        first_send[p, :, 3 * slots : 4 * slots] = high.astype(F32)
    first_recv[0] = first_send[my_win]
    held[0] = kern_ref[my_win, pl.ds(pl.multiple_of(my_off * part, 8), part), :]

    pl.semaphore_wait(barrier, total - 1)

    @pl.loop(1, total)
    def _(k):
        dest = to_of(k)
        pltpu.make_async_remote_copy(
            src_ref=first_send.at[dest // offs], dst_ref=first_recv.at[k],
            send_sem=send_sem.at[0], recv_sem=recv_sem.at[0],
            device_id=place(dest), device_id_type=MESH,
        ).start()

    @pl.loop(1, total)
    def _(k):
        dest = to_of(k)
        half = pl.ds(pl.multiple_of(lax.rem(dest, offs) * part, 8), part)
        pltpu.make_async_remote_copy(
            src_ref=kern_ref.at[dest // offs, half, :], dst_ref=held.at[k],
            send_sem=kern_send, recv_sem=kern_recv.at[k // GROUP],
            device_id=place(dest), device_id_type=MESH,
        ).start()

    def bytes_in(ref, sem):
        pltpu.make_async_copy(ref, ref, sem).wait()

    def cat(pieces):
        return jnp.concatenate(pieces, axis=1)

    def highs(g):
        return cat([first_recv[g * GROUP + i, :, 3 * slots : 4 * slots] for i in range(GROUP)])

    def kern_of(g):
        return cat([held[g * GROUP + i] for i in range(GROUP)])

    def scatter_group(g, weight_of, scale):
        row = cat([weight_of(g * GROUP + i) for i in range(GROUP)]) / scale
        top, rest = split2(kern_of(g) * row)
        both = jnp.concatenate([top, rest], axis=0)
        high = jnp.broadcast_to(highs(g), both.shape)
        left = jnp.concatenate(
            [both * jnp.where(high == h, 1.0, 0.0).astype(BF16) for h in range(HIGH)], axis=0
        )
        acc[...] += lax.dot_general(left, low1h[g], (((1,), (1,)), ((), ())), preferred_element_type=F32)

    def collect(h):
        at = h * 2 * part
        return acc[at : at + part, :] + acc[at + part : at + 2 * part, :]

    def forward(step):
        square = jnp.zeros((part, LOW), F32)
        lefts = []
        for h in range(HIGH):
            piece = raw[h]
            square += piece * piece
            lefts += list(split2(piece))
        left = jnp.concatenate(lefts, axis=0)
        norm = fold(jnp.sum(square, axis=0, keepdims=True))

        @pl.loop(0, groups)
        def _(g):
            got = jnp.dot(left, low1h[g], preferred_element_type=F32)
            high = jnp.broadcast_to(highs(g), (part, width))
            fetched = jnp.zeros((part, width), F32)
            for h in range(HIGH):
                at = h * 2 * part
                fetched += jnp.where(high == h, got[at : at + part] + got[at + part : at + 2 * part], 0.0)
            values = jnp.sum(fetched * kern_of(g), axis=0, keepdims=True)
            for i in range(GROUP):
                f_send[step, g * GROUP + i, :, 0:slots] = values[:, i * slots : (i + 1) * slots]
                f_send[step, g * GROUP + i, :, slots : 2 * slots] = norm

        @pl.loop(1, total)
        def _(k):
            pltpu.make_async_remote_copy(
                src_ref=f_send.at[step, k], dst_ref=f_recv.at[step, me],
                send_sem=send_sem.at[1 + 2 * step], recv_sem=recv_sem.at[1 + 2 * step],
                device_id=place(from_of(k)), device_id_type=MESH,
            ).start()

        f_recv[step, me] = f_send[step, 0]
        bytes_in(f_recv.at[step, pl.ds(1, total - 1)], recv_sem.at[1 + 2 * step])

    bytes_in(first_recv.at[pl.ds(1, total - 1)], recv_sem.at[0])
    beta = jnp.sqrt(total_of(first_recv[:, :, slots : 2 * slots]))
    low_iota = lax.broadcasted_iota(jnp.int32, (LOW, slots), 0).astype(F32)

    @pl.loop(0, groups)
    def _(g):
        for i in range(GROUP):
            low = first_recv[g * GROUP + i, :, 2 * slots : 3 * slots]
            low1h[g, :, i * slots : (i + 1) * slots] = jnp.where(low_iota == low, 1.0, 0.0).astype(BF16)

    acc[...] = jnp.zeros_like(acc)
    first_weight = lambda k: first_recv[k, :, 0:slots]
    bytes_in(held.at[pl.ds(1, GROUP - 1)], kern_recv.at[0])
    scatter_group(0, first_weight, beta)

    @pl.loop(1, groups)
    def _(g):
        bytes_in(held.at[pl.ds(g * GROUP, GROUP)], kern_recv.at[g])
        scatter_group(g, first_weight, beta)

    for h in range(HIGH):
        raw[h] = collect(h)
    data = data / beta

    phibar = beta
    rhobar = theta_rho = sine = cosine = None
    for step in range(ITERS):
        forward(step)
        alpha = jnp.sqrt(total_of(f_recv[step, :, :, slots : 2 * slots]))
        terms = cat([
            sum(f_recv[step, p * offs + o, :, 0:slots] for o in range(offs)) for p in range(wins)
        ])
        data = gather_rays(terms) / alpha - alpha * data
        partial = fold(data * data)
        last = step == ITERS - 1
        if not last:
            weights = take(data)
            for p in range(wins):
                w_send[step, p, :, 0:slots] = weights[:, p * slots : (p + 1) * slots]
                w_send[step, p, :, slots : 2 * slots] = partial
        else:
            s_send[...] = partial

        @pl.loop(1, total)
        def _(k):
            dest = to_of(k)
            pltpu.make_async_remote_copy(
                src_ref=s_send if last else w_send.at[step, dest // offs],
                dst_ref=s_recv.at[k] if last else w_recv.at[step, k],
                send_sem=send_sem.at[2 + 2 * step], recv_sem=recv_sem.at[2 + 2 * step],
                device_id=place(dest), device_id_type=MESH,
            ).start()

        if step == 0:
            rhobar = alpha
        else:
            theta_rho = sine * alpha / rho
            rhobar = -cosine * alpha
        for h in range(HIGH):
            fresh = raw[h] / alpha
            vec[h] = fresh
            srch[my_off, h] = fresh if step == 0 else fresh - theta_rho * srch[my_off, h]
        if last:
            for other in range(1, offs):
                for which, ref in enumerate((upd, srch)):
                    pltpu.make_async_remote_copy(
                        src_ref=ref.at[my_off], dst_ref=ref.at[my_off],
                        send_sem=pair_send.at[which, other], recv_sem=pair_recv.at[which, other],
                        device_id=(lax.rem(my_off + other, offs), my_win), device_id_type=MESH,
                    ).start()
            s_recv[0] = s_send[...]
            bytes_in(s_recv.at[pl.ds(1, total - 1)], recv_sem.at[2 + 2 * step])
            beta = jnp.sqrt(total_of(s_recv[...]))
        else:
            w_recv[step, 0] = w_send[step, my_win]
            bytes_in(w_recv.at[step, pl.ds(1, total - 1)], recv_sem.at[2 + 2 * step])
            beta = jnp.sqrt(total_of(w_recv[step, :, :, slots : 2 * slots]))

        data = data / beta
        rho = jnp.sqrt(rhobar * rhobar + beta * beta)
        cosine = rhobar / rho
        sine = beta / rho
        phi = cosine * phibar
        phibar = sine * phibar
        if last:
            data_ref[...] = data
            for other in range(1, offs):
                for which, ref in enumerate((upd, srch)):
                    bytes_in(ref.at[0], pair_recv.at[which, other])
            for o in range(offs):
                for h in range(HIGH):
                    out_ref[o * part : (o + 1) * part, h * LOW : (h + 1) * LOW] = (
                        upd[o, h] + phi / rho * srch[o, h]
                    )
        else:
            acc[...] = jnp.zeros_like(acc)

            @pl.loop(0, groups)
            def _(g):
                scatter_group(g, lambda k: w_recv[step, k, :, 0:slots], beta)

            for h in range(HIGH):
                raw[h] = collect(h) - beta * vec[h]
                moved = phi / rho * srch[my_off, h]
                upd[my_off, h] = moved if step == 0 else upd[my_off, h] + moved

    bytes_in(first_recv.at[pl.ds(1, total - 1)], send_sem.at[0])
    bytes_in(held.at[pl.ds(1, total - 1)], kern_send)
    for step in range(ITERS):
        bytes_in(f_recv.at[step, pl.ds(1, total - 1)], send_sem.at[1 + 2 * step])
        if step < ITERS - 1:
            bytes_in(w_recv.at[step, pl.ds(1, total - 1)], send_sem.at[2 + 2 * step])
        else:
            bytes_in(s_recv.at[pl.ds(1, total - 1)], send_sem.at[2 + 2 * step])
    for other in range(1, offs):
        for which, ref in enumerate((upd, srch)):
            bytes_in(ref.at[0], pair_send.at[which, other])


def body(kernels, blocks, counts, ray_of, slopes):
    offs, wins = lax.axis_size("off"), lax.axis_size("win")
    total = offs * wins
    cells, slots = kernels.shape[3:]
    rays = slopes.shape[2]
    part = cells // offs
    groups = total // GROUP
    vmem = pl.BlockSpec(memory_space=pltpu.VMEM)
    model = (HIGH, part, LOW)
    update, data = pl.pallas_call(
        functools.partial(kernel, offs, wins),
        out_shape=(
            jax.ShapeDtypeStruct((cells, BLK_DEV), F32),
            jax.ShapeDtypeStruct((1, rays), F32),
        ),
        in_specs=[vmem, vmem, pl.BlockSpec(memory_space=pltpu.SMEM), vmem, vmem],
        out_specs=(vmem, vmem),
        scratch_shapes=[
            pltpu.VMEM((rays, wins * slots), BF16),
            pltpu.VMEM((groups, LOW, GROUP * slots), BF16),
            pltpu.VMEM((total, part, slots), F32),
            pltpu.VMEM((wins, 1, 4 * slots), F32),
            pltpu.VMEM((total, 1, 4 * slots), F32),
            pltpu.VMEM((ITERS - 1, wins, 1, 2 * slots), F32),
            pltpu.VMEM((ITERS - 1, total, 1, 2 * slots), F32),
            pltpu.VMEM((ITERS, total, 1, 2 * slots), F32),
            pltpu.VMEM((ITERS, total, 1, 2 * slots), F32),
            pltpu.VMEM((1, slots), F32),
            pltpu.VMEM((total, 1, slots), F32),
            pltpu.VMEM((HIGH * 2 * part, LOW), F32),
            pltpu.VMEM(model, F32),
            pltpu.VMEM(model, F32),
            pltpu.VMEM((offs,) + model, F32),
            pltpu.VMEM((offs,) + model, F32),
            pltpu.SemaphoreType.DMA((2 * ITERS + 1,)),
            pltpu.SemaphoreType.DMA((2 * ITERS + 1,)),
            pltpu.SemaphoreType.DMA,
            pltpu.SemaphoreType.DMA((groups,)),
            pltpu.SemaphoreType.DMA((2, offs)),
            pltpu.SemaphoreType.DMA((2, offs)),
        ],
        compiler_params=pltpu.CompilerParams(
            collective_id=0, has_side_effects=True, vmem_limit_bytes=48 * 1024 * 1024
        ),
    )(kernels[0, 0], blocks[0, 0], counts[0, 0], ray_of[0, 0], slopes[0])
    return update, data[None]


def solution(mesh):
    in_specs = (
        P("off", "win", None, None, None),
        P("off", "win", None, None),
        P("off", "win", None),
        P("off", "win", None, None),
        P("off", "win", None),
    )
    out_specs = (P(None, "win"), P("off", "win", None))
    return jax.shard_map(body, mesh=mesh, in_specs=in_specs, out_specs=out_specs, check_vma=False)
```

time: 633 us -> 73.7 us (0.12)
  blocking collectives: 329 us -> 0 us
  other arithmetic: 101 us -> 0 us
  waiting for transfers between devices: 81.7 us -> 0 us
  local copies, waits for them, and re-layouts: 84.1 us -> 4.48 us
  Pallas kernels: 0 us -> 68.3 us
  between operations: 19.4 us -> 0.66 us
  starting transfers between devices: 16.3 us -> 0 us
    psum x7 -> x0, blocking collectives: 286 us -> none  [the longest x4 158 us: data_norm(): return lax.psum(jnp.sum(vector * vector), ('off', 'win'))]
    scatter-add x6 -> x0, other arithmetic: 82.6 us -> none  [the longest x3 44.4 us: body(): jax.ops.segment_sum(returned.reshape(-1), ray_flat, num_segments=ray_count)]
    gather x9 -> x0, local copies, waits for them, and re-layouts: 76.6 us -> none  [the longest x3 48.5 us: residual_weights(): return data.reshape(-1)[ray_of]]
    pallas_call x0 -> x1, Pallas kernels: none -> 68.3 us  [body(): pl.pallas_call(functools.partial(kernel, offs, wins), out_shape=(jax.Shap...]
    psum x3 -> x0, waiting for transfers between devices: 50.2 us -> none  [accumulate(): return lax.psum(local, 'off')]
    all_to_all x4 -> x0, blocking collectives: 43.6 us -> none  [the longest x2 23.9 us: adjoint(): lax.all_to_all(residual_weights(data), 'win', split_axis=2, concat_axis=1...]
    all_to_all x4 -> x0, waiting for transfers between devices: 31.5 us -> none  [the longest x1 11.9 us: body(): lax.all_to_all(masked, 'win', split_axis=2, concat_axis=1, tiled=True)]
    all_to_all x4 -> x0, starting transfers between devices: 16.1 us -> none  [the longest x1 5.61 us: adjoint(): lax.all_to_all(residual_weights(data), 'win', split_axis=2, concat_axis=1...]
  transfers between devices with their start and end apart: 7 -> 0, of which waited for: 7 -> 0; matrix products, arithmetic and copies ran while one was open for 0% -> 0% of each run, Pallas kernels for 0% -> 0%
where the time goes in v1:
time: 73.7 us; the launch traced here: 73.4 us
  Pallas kernels  68.3 us (93%)
  local copies, waits for them, and re-layouts  4.48 us (6%)
    pallas_call x1, Pallas kernels, body(): pl.pallas_call(functools.partial(kernel, offs, wins), out_shape=(jax.Shap...  68.3 us
    unnamed x12, local copies, waits for them, and re-layouts  4.48 us

profile of v1, /device:TPU:0, one launch (start us, length us, event | category | flops | bytes accessed | tf_op | source)
XLA Modules:
  0.0 73.4 jit_solution(15168344565756270302)
XLA Ops:
  0.6 0.0 copy-start.1
  0.6 0.0 copy-start.4
  0.7 0.7 copy-done.1
  1.3 0.0 copy-done.4
  1.3 0.0 copy-start
  1.3 1.0 %copy-done = f32[1,1,16,64,128]{4,3,2,1,0:T(8,128)S(1)} copy-done((f32[1,1,16,64,128]{4,3,2,1,0:T(8,128)S(1)}, f32[1,1,16,64,128]{4,3,2,1,0:T(8,128)}, u32[]{:S(2)}) %copy-start) | copy-done | bytes 524312
  2.4 0.0 copy-start.2
  2.4 0.7 copy-done.2
  3.1 0.0 copy-start.3
  3.1 0.7 copy-done.3
  3.8 68.3 %shard_map.68 = (f32[64,2048]{1,0:T(8,128)S(1)}, f32[1,512]{1,0:T(1,128)S(1)}) custom-call(f32[16,64,128]{2,1,0:T(8,128)S(1)} %bitcast.6, s32[16,128]{1,0:T(8,128)S(1)} %bitcast.7, s32[16]{0:T(128)S(1)} %bitcast.11, s32[16,128]{1,0:T(8,128)S(1)} %bitcast.8, f32[1,512]{1,0:T(1,128)S(1)} %bitcast.9), custom_call_target="tpu_custom_call" | custom-call | tf_op jit(solution)/shard_map/pallas_call | solution.py:314
  72.0 0.8 %copy.9 = f32[64,2048]{1,0:T(8,128)} copy(f32[64,2048]{1,0:T(8,128)S(1)} %get-tuple-element.8) | data formatting | bytes 1048576
  72.8 0.6 copy.10
Async XLA Ops:
  0.6 0.7 copy-start.1
  0.6 0.7 copy-start.4
  1.3 1.0 %copy-start = (f32[1,1,16,64,128]{4,3,2,1,0:T(8,128)S(1)}, f32[1,1,16,64,128]{4,3,2,1,0:T(8,128)}, u32[]{:S(2)}) copy-start(f32[1,1,16,64,128]{4,3,2,1,0:T(8,128)} %param.5) | copy-start | bytes 1572868
  2.4 0.7 copy-start.2
  3.1 0.7 copy-start.3

commit v2 on v1

v2 whole, which is shorter than its diff:
```python
import functools

import jax
import jax.numpy as jnp
from jax import lax
from jax.experimental import pallas as pl
from jax.experimental.pallas import tpu as pltpu
from jax.sharding import PartitionSpec as P

BLK_DEV = 2048
ITERS = 3
LOW = 256
HIGH = BLK_DEV // LOW
GROUP = 8
LANES = 128

F32 = jnp.float32
BF16 = jnp.bfloat16
MESH = pl.DeviceIdType.MESH


def split2(x):
    top = x.astype(BF16)
    rest = (x - top.astype(F32)).astype(BF16)
    return top, rest


def rows_of(x):
    a = x.astype(BF16).astype(F32)
    b = (x - a).astype(BF16).astype(F32)
    c = x - a - b
    shape = (8, x.shape[1])
    i = lax.broadcasted_iota(jnp.int32, shape, 0)
    wide = lambda y: jnp.broadcast_to(y, shape)
    zero = jnp.zeros(shape, F32)
    return jnp.where(i == 0, wide(a), jnp.where(i == 1, wide(b), jnp.where(i == 2, wide(c), zero)))


def fold(x):
    return sum(x[:, i : i + LANES] for i in range(0, x.shape[1], LANES))


def kernel(
    offs, wins, kern_hbm, block_hbm, count_hbm, ray_hbm, slope_hbm,
    out_ref, data_ref,
    block_ref, count_ref, ray_ref, slope_ref,
    rays1h, ray_high, low1h, high1h, held,
    first_send, first_recv, w_send, w_recv, f_send, f_recv, s_send, s_recv,
    acc, vec, raw, upd, srch,
    send_sem, recv_sem, kern_send, kern_recv, pair_send, pair_recv, load_sem,
):
    total = offs * wins
    part = kern_hbm.shape[1] // offs
    slots = kern_hbm.shape[2]
    ray_low = rays1h.shape[0]
    ray_parts = slope_ref.shape[1] // ray_low
    groups = total // GROUP
    width = GROUP * slots
    step_wins = GROUP // offs
    my_off = lax.axis_index("off")
    my_win = lax.axis_index("win")
    me = my_win * offs + my_off
    half = lambda o: pl.ds(pl.multiple_of(o * part, 8), part)
    off_to = [lax.rem(my_off + d, offs) for d in range(offs)]
    off_from = [lax.rem(my_off + offs - d, offs) for d in range(offs)]
    win_to = lambda d: lax.rem(my_win + d, wins)
    win_from = lambda d: lax.rem(my_win + wins - d, wins)

    def group_pairs(g):
        return [(i, g * step_wins + i // offs, i % offs) for i in range(GROUP)]

    def each_group(act):
        act(0, True)

        @pl.loop(1, groups)
        def _(g):
            act(g, False)

    loads = [
        pltpu.make_async_copy(src, dst, load_sem.at[i])
        for i, (src, dst) in enumerate(
            ((count_hbm, count_ref), (ray_hbm, ray_ref), (slope_hbm, slope_ref), (block_hbm, block_ref))
        )
    ]
    loads.append(pltpu.make_async_copy(kern_hbm.at[my_win, half(my_off), :], held.at[0], load_sem.at[4]))
    for load in loads:
        load.start()

    barrier = pltpu.get_barrier_semaphore()

    def greet(g, first):
        for i, dw, do in group_pairs(g):
            if not (first and i == 0):
                pl.semaphore_signal(
                    barrier, inc=1, device_id=(off_to[do], win_to(dw)), device_id_type=MESH
                )

    each_group(greet)
    for load in loads:
        load.wait()

    ray_iota = lax.broadcasted_iota(jnp.int32, (ray_low, slots), 0)
    lane = lax.broadcasted_iota(jnp.int32, (1, slots), 1)
    for p in range(wins):
        ids = ray_ref[p : p + 1, :]
        high = ids // ray_low
        low = jnp.where(lane < count_ref[p], ids - high * ray_low, -1)
        rays1h[:, p * slots : (p + 1) * slots] = jnp.where(ray_iota == low, 1.0, 0.0).astype(BF16)
        ray_high[:, p * slots : (p + 1) * slots] = jnp.broadcast_to(high, (8, slots))

    def cat(pieces):
        return jnp.concatenate(pieces, axis=1)

    def take(data):
        left = jnp.concatenate(
            [rows_of(data[:, r * ray_low : (r + 1) * ray_low]) for r in range(ray_parts)], axis=0
        ).astype(BF16)
        got = jnp.dot(left, rays1h[...], preferred_element_type=F32)
        high = ray_high[...]
        picked = sum(jnp.where(high == r, got[8 * r : 8 * r + 8], 0.0) for r in range(ray_parts))
        return jnp.sum(picked, axis=0, keepdims=True)

    def gather_rays(values):
        rows = rows_of(values)
        high = ray_high[...]
        left = jnp.concatenate(
            [jnp.where(high == r, rows, 0.0) for r in range(ray_parts)], axis=0
        ).astype(BF16)
        got = lax.dot_general(left, rays1h[...], (((1,), (1,)), ((), ())), preferred_element_type=F32)
        return cat([jnp.sum(got[8 * r : 8 * r + 8], axis=0, keepdims=True) for r in range(ray_parts)])

    def total_of(partials):
        return jnp.sum(jnp.sum(partials, axis=0), axis=1, keepdims=True)

    data = slope_ref[...]
    weights = take(data)
    partial = fold(data * data)
    for p in range(wins):
        ids = block_ref[p : p + 1, :]
        high = ids // LOW
        first_send[p, :, 0:slots] = weights[:, p * slots : (p + 1) * slots]
        first_send[p, :, slots : 2 * slots] = partial
        first_send[p, :, 2 * slots : 3 * slots] = (ids - high * LOW).astype(F32)
        first_send[p, :, 3 * slots : 4 * slots] = high.astype(F32)
    first_recv[0] = first_send[my_win]

    pl.semaphore_wait(barrier, total - 1)

    def to_owners(source_of, target_of, index):
        def send(g, first):
            for i, dw, do in group_pairs(g):
                if not (first and i == 0):
                    win = win_to(dw)
                    pltpu.make_async_remote_copy(
                        src_ref=source_of(win), dst_ref=target_of(g * GROUP + i),
                        send_sem=send_sem.at[index], recv_sem=recv_sem.at[index],
                        device_id=(off_to[do], win), device_id_type=MESH,
                    ).start()

        each_group(send)

    to_owners(lambda win: first_send.at[win], lambda k: first_recv.at[k], 0)

    def send_rows(g, first):
        for i, dw, do in group_pairs(g):
            if not (first and i == 0):
                win = win_to(dw)
                pltpu.make_async_remote_copy(
                    src_ref=kern_hbm.at[win, half(off_to[do]), :], dst_ref=held.at[g * GROUP + i],
                    send_sem=kern_send, recv_sem=kern_recv.at[g],
                    device_id=(off_to[do], win), device_id_type=MESH,
                ).start()

    each_group(send_rows)

    def bytes_in(ref, sem):
        pltpu.make_async_copy(ref, ref, sem).wait()

    def kern_of(g):
        return cat([held[g * GROUP + i] for i in range(GROUP)])

    def scatter_group(g, weight_of, scale):
        row = cat([weight_of(g * GROUP + i) for i in range(GROUP)]) / scale
        parts = split2(kern_of(g) * row)
        rows = []
        for h in range(HIGH):
            mask = jnp.concatenate([high1h[g, h]] * (part // 16), axis=0)
            rows.append(cat([piece * mask for piece in parts]))
        left = jnp.concatenate(rows, axis=0)
        low = low1h[g]
        acc[...] += lax.dot_general(
            left, cat([low, low]), (((1,), (1,)), ((), ())), preferred_element_type=F32
        )

    def collect(h):
        return acc[h * part : (h + 1) * part, :]

    def forward(step):
        square = jnp.zeros((part, LOW), F32)
        lefts = []
        for h in range(HIGH):
            piece = raw[h]
            square += piece * piece
            lefts.append(cat(split2(piece)))
        left = jnp.concatenate(lefts, axis=0)
        norm = fold(jnp.sum(square, axis=0, keepdims=True))

        def terms_of(g, first):
            low = low1h[g]
            got = jnp.dot(left, jnp.concatenate([low, low], axis=0), preferred_element_type=F32)
            high = jnp.broadcast_to(
                cat([first_recv[g * GROUP + i, :, 3 * slots : 4 * slots] for i in range(GROUP)]), (8, width)
            )
            fetched = [jnp.zeros((8, width), F32)] * (part // 8)
            for h in range(HIGH):
                hit = high == h
                for r in range(part // 8):
                    at = h * part + r * 8
                    fetched[r] = jnp.where(hit, got[at : at + 8], fetched[r])
            rows = kern_of(g)
            mixed = sum(fetched[r] * rows[r * 8 : r * 8 + 8] for r in range(part // 8))
            values = jnp.sum(mixed, axis=0, keepdims=True)
            for i, dw, do in group_pairs(g):
                k = g * GROUP + i
                f_send[step, k, :, 0:slots] = values[:, i * slots : (i + 1) * slots]
                f_send[step, k, :, slots : 2 * slots] = norm
                if first and i == 0:
                    f_recv[step, me] = f_send[step, 0]
                else:
                    pltpu.make_async_remote_copy(
                        src_ref=f_send.at[step, k], dst_ref=f_recv.at[step, me],
                        send_sem=send_sem.at[1 + 2 * step], recv_sem=recv_sem.at[1 + 2 * step],
                        device_id=(off_from[do], win_from(dw)), device_id_type=MESH,
                    ).start()

        each_group(terms_of)
        bytes_in(f_recv.at[step, pl.ds(1, total - 1)], recv_sem.at[1 + 2 * step])

    bytes_in(first_recv.at[pl.ds(1, total - 1)], recv_sem.at[0])
    beta = jnp.sqrt(total_of(first_recv[:, :, slots : 2 * slots]))
    low_iota = lax.broadcasted_iota(jnp.int32, (LOW, slots), 0).astype(F32)

    @pl.loop(0, groups)
    def _(g):
        for i in range(GROUP):
            here = pl.ds(i * slots, slots)
            low = first_recv[g * GROUP + i, :, 2 * slots : 3 * slots]
            low1h[g, :, here] = jnp.where(low_iota == low, 1.0, 0.0).astype(BF16)
            high = jnp.broadcast_to(first_recv[g * GROUP + i, :, 3 * slots : 4 * slots], (16, slots))
            for h in range(HIGH):
                high1h[g, h, :, here] = jnp.where(high == h, 1.0, 0.0).astype(BF16)

    acc[...] = jnp.zeros_like(acc)

    def first_adjoint(g, first):
        begin = 1 if first else 0
        bytes_in(held.at[pl.ds(g * GROUP + begin, GROUP - begin)], kern_recv.at[g])
        scatter_group(g, lambda k: first_recv[k, :, 0:slots], beta)

    each_group(first_adjoint)

    for h in range(HIGH):
        raw[h] = collect(h)
    data = data / beta

    phibar = beta
    rho = rhobar = sine = cosine = None
    for step in range(ITERS):
        forward(step)
        alpha = jnp.sqrt(total_of(f_recv[step, :, :, slots : 2 * slots]))
        terms = cat([
            sum(f_recv[step, p * offs + o, :, 0:slots] for o in range(offs)) for p in range(wins)
        ])
        data = gather_rays(terms) / alpha - alpha * data
        partial = fold(data * data)
        last = step == ITERS - 1
        index = 2 + 2 * step
        if not last:
            weights = take(data)
            for p in range(wins):
                w_send[step, p, :, 0:slots] = weights[:, p * slots : (p + 1) * slots]
                w_send[step, p, :, slots : 2 * slots] = partial
            to_owners(lambda win: w_send.at[step, win], lambda k: w_recv.at[step, k], index)
        else:
            s_send[...] = partial
            to_owners(lambda win: s_send, lambda k: s_recv.at[k], index)

        if step == 0:
            rhobar = alpha
        else:
            theta_rho = sine * alpha / rho
            rhobar = -cosine * alpha
        for h in range(HIGH):
            fresh = raw[h] / alpha
            vec[h] = fresh
            srch[my_off, h] = fresh if step == 0 else fresh - theta_rho * srch[my_off, h]
        if last:
            for other in range(1, offs):
                for which, ref in enumerate((upd, srch)):
                    pltpu.make_async_remote_copy(
                        src_ref=ref.at[my_off], dst_ref=ref.at[my_off],
                        send_sem=pair_send.at[which, other], recv_sem=pair_recv.at[which, other],
                        device_id=(off_to[other], my_win), device_id_type=MESH,
                    ).start()
            s_recv[0] = s_send[...]
            bytes_in(s_recv.at[pl.ds(1, total - 1)], recv_sem.at[index])
            beta = jnp.sqrt(total_of(s_recv[...]))
        else:
            acc[...] = jnp.zeros_like(acc)
            w_recv[step, 0] = w_send[step, my_win]
            bytes_in(w_recv.at[step, pl.ds(1, total - 1)], recv_sem.at[index])
            beta = jnp.sqrt(total_of(w_recv[step, :, :, slots : 2 * slots]))

        data = data / beta
        rho = jnp.sqrt(rhobar * rhobar + beta * beta)
        cosine = rhobar / rho
        sine = beta / rho
        phi = cosine * phibar
        phibar = sine * phibar
        if last:
            data_ref[...] = data
            for other in range(1, offs):
                for which, ref in enumerate((upd, srch)):
                    bytes_in(ref.at[0], pair_recv.at[which, other])
            for o in range(offs):
                for h in range(HIGH):
                    out_ref[o * part : (o + 1) * part, h * LOW : (h + 1) * LOW] = (
                        upd[o, h] + phi / rho * srch[o, h]
                    )
        else:
            @pl.loop(0, groups)
            def _(g):
                scatter_group(g, lambda k: w_recv[step, k, :, 0:slots], beta)

            for h in range(HIGH):
                raw[h] = collect(h) - beta * vec[h]
                moved = phi / rho * srch[my_off, h]
                upd[my_off, h] = moved if step == 0 else upd[my_off, h] + moved

    bytes_in(first_recv.at[pl.ds(1, total - 1)], send_sem.at[0])
    bytes_in(held.at[pl.ds(1, total - 1)], kern_send)
    for step in range(ITERS):
        bytes_in(f_recv.at[step, pl.ds(1, total - 1)], send_sem.at[1 + 2 * step])
        if step < ITERS - 1:
            bytes_in(w_recv.at[step, pl.ds(1, total - 1)], send_sem.at[2 + 2 * step])
        else:
            bytes_in(s_recv.at[pl.ds(1, total - 1)], send_sem.at[2 + 2 * step])
    for other in range(1, offs):
        for which, ref in enumerate((upd, srch)):
            bytes_in(ref.at[0], pair_send.at[which, other])


def body(kernels, blocks, counts, ray_of, slopes):
    offs, wins = lax.axis_size("off"), lax.axis_size("win")
    total = offs * wins
    cells, slots = kernels.shape[3:]
    rays = slopes.shape[2]
    part = cells // offs
    groups = total // GROUP
    ray_low = LOW if rays % LOW == 0 else rays
    vmem = pl.BlockSpec(memory_space=pltpu.VMEM)
    model = (HIGH, part, LOW)
    update, data = pl.pallas_call(
        functools.partial(kernel, offs, wins),
        out_shape=(
            jax.ShapeDtypeStruct((cells, BLK_DEV), F32),
            jax.ShapeDtypeStruct((1, rays), F32),
        ),
        in_specs=[pl.BlockSpec(memory_space=pl.ANY)] * 5,
        out_specs=(vmem, vmem),
        scratch_shapes=[
            pltpu.VMEM((wins, slots), jnp.int32),
            pltpu.SMEM((wins,), jnp.int32),
            pltpu.VMEM((wins, slots), jnp.int32),
            pltpu.VMEM((1, rays), F32),
            pltpu.VMEM((ray_low, wins * slots), BF16),
            pltpu.VMEM((8, wins * slots), jnp.int32),
            pltpu.VMEM((groups, LOW, GROUP * slots), BF16),
            pltpu.VMEM((groups, HIGH, 16, GROUP * slots), BF16),
            pltpu.VMEM((total, part, slots), F32),
            pltpu.VMEM((wins, 1, 4 * slots), F32),
            pltpu.VMEM((total, 1, 4 * slots), F32),
            pltpu.VMEM((ITERS - 1, wins, 1, 2 * slots), F32),
            pltpu.VMEM((ITERS - 1, total, 1, 2 * slots), F32),
            pltpu.VMEM((ITERS, total, 1, 2 * slots), F32),
            pltpu.VMEM((ITERS, total, 1, 2 * slots), F32),
            pltpu.VMEM((1, slots), F32),
            pltpu.VMEM((total, 1, slots), F32),
            pltpu.VMEM((HIGH * part, LOW), F32),
            pltpu.VMEM(model, F32),
            pltpu.VMEM(model, F32),
            pltpu.VMEM((offs,) + model, F32),
            pltpu.VMEM((offs,) + model, F32),
            pltpu.SemaphoreType.DMA((2 * ITERS + 1,)),
            pltpu.SemaphoreType.DMA((2 * ITERS + 1,)),
            pltpu.SemaphoreType.DMA,
            pltpu.SemaphoreType.DMA((groups,)),
            pltpu.SemaphoreType.DMA((2, offs)),
            pltpu.SemaphoreType.DMA((2, offs)),
            pltpu.SemaphoreType.DMA((5,)),
        ],
        compiler_params=pltpu.CompilerParams(
            collective_id=0, has_side_effects=True, vmem_limit_bytes=48 * 1024 * 1024
        ),
    )(kernels[0, 0], blocks[0, 0], counts[0, 0], ray_of[0, 0], slopes[0])
    return update, data[None]


def solution(mesh):
    in_specs = (
        P("off", "win", None, None, None),
        P("off", "win", None, None),
        P("off", "win", None),
        P("off", "win", None, None),
        P("off", "win", None),
    )
    out_specs = (P(None, "win"), P("off", "win", None))
    return jax.shard_map(body, mesh=mesh, in_specs=in_specs, out_specs=out_specs, check_vma=False)
```

time: 73.7 us -> 66 us (0.90)
  Pallas kernels: 68.3 us -> 60.6 us
    pallas_call x1, Pallas kernels: 68.3 us -> 60.6 us  [body(): pl.pallas_call(functools.partial(kernel, offs, wins), out_shape=(jax.Shap...]
where the time goes in v2:
time: 66 us; the launch traced here: 65.7 us
  Pallas kernels  60.6 us (92%)
  local copies, waits for them, and re-layouts  4.48 us (7%)
  between operations  0.66 us (1%)
    pallas_call x1, Pallas kernels, body(): pl.pallas_call(functools.partial(kernel, offs, wins), out_shape=(jax.Shap...  60.6 us
    unnamed x12, local copies, waits for them, and re-layouts  4.48 us

profile of v2, /device:TPU:0, one launch (start us, length us, event | category | flops | bytes accessed | tf_op | source)
XLA Modules:
  0.0 65.7 jit_solution(7001844282340658127)
XLA Ops:
  0.6 0.0 copy-start.1
  0.6 0.0 copy-start.4
  0.7 0.7 %copy-done.1 = s32[1,1,16,128]{3,2,1,0:T(8,128)S(1)} copy-done((s32[1,1,16,128]{3,2,1,0:T(8,128)S(1)}, s32[1,1,16,128]{3,2,1,0:T(8,128)}, u32[]{:S(2)}) %copy-start.1) | copy-done | bytes 8216
  1.3 0.0 copy-done.4
  1.3 0.0 copy-start
  1.3 1.0 %copy-done = f32[1,1,16,64,128]{4,3,2,1,0:T(8,128)S(1)} copy-done((f32[1,1,16,64,128]{4,3,2,1,0:T(8,128)S(1)}, f32[1,1,16,64,128]{4,3,2,1,0:T(8,128)}, u32[]{:S(2)}) %copy-start) | copy-done | bytes 524312
  2.4 0.0 copy-start.2
  2.4 0.7 %copy-done.2 = s32[1,1,16,128]{3,2,1,0:T(8,128)S(1)} copy-done((s32[1,1,16,128]{3,2,1,0:T(8,128)S(1)}, s32[1,1,16,128]{3,2,1,0:T(8,128)}, u32[]{:S(2)}) %copy-start.2) | copy-done | bytes 8216
  3.1 0.0 copy-start.3
  3.1 0.7 %copy-done.3 = f32[1,1,512]{2,1,0:T(1,128)S(1)} copy-done((f32[1,1,512]{2,1,0:T(1,128)S(1)}, f32[1,1,512]{2,1,0:T(1,128)}, u32[]{:S(2)}) %copy-start.3) | copy-done | bytes 2072
  3.8 60.6 %shard_map.68 = (f32[64,2048]{1,0:T(8,128)S(1)}, f32[1,512]{1,0:T(1,128)S(1)}) custom-call(f32[16,64,128]{2,1,0:T(8,128)S(1)} %bitcast.6, s32[16,128]{1,0:T(8,128)S(1)} %bitcast.7, s32[16]{0:T(128)S(1)} %bitcast.11, s32[16,128]{1,0:T(8,128)S(1)} %bitcast.8, f32[1,512]{1,0:T(1,128)S(1)} %bitcast.9), custom_call_target="tpu_custom_call" | custom-call | tf_op jit(solution)/shard_map/pallas_call | solution.py:363
  64.3 0.8 %copy.9 = f32[64,2048]{1,0:T(8,128)} copy(f32[64,2048]{1,0:T(8,128)S(1)} %get-tuple-element.8) | data formatting | bytes 1048576
  65.1 0.6 copy.10
Async XLA Ops:
  0.6 0.7 %copy-start.1 = (s32[1,1,16,128]{3,2,1,0:T(8,128)S(1)}, s32[1,1,16,128]{3,2,1,0:T(8,128)}, u32[]{:S(2)}) copy-start(s32[1,1,16,128]{3,2,1,0:T(8,128)} %param.6) | copy-start | bytes 24580
  0.6 0.7 %copy-start.4 = (s32[1,1,16]{2,1,0:T(1,128)S(1)}, s32[1,1,16]{2,1,0:T(1,128)}, u32[]{:S(2)}) copy-start(s32[1,1,16]{2,1,0:T(1,128)} %param.7) | copy-start | bytes 196
  1.3 1.0 %copy-start = (f32[1,1,16,64,128]{4,3,2,1,0:T(8,128)S(1)}, f32[1,1,16,64,128]{4,3,2,1,0:T(8,128)}, u32[]{:S(2)}) copy-start(f32[1,1,16,64,128]{4,3,2,1,0:T(8,128)} %param.5) | copy-start | bytes 1572868
  2.4 0.7 %copy-start.2 = (s32[1,1,16,128]{3,2,1,0:T(8,128)S(1)}, s32[1,1,16,128]{3,2,1,0:T(8,128)}, u32[]{:S(2)}) copy-start(s32[1,1,16,128]{3,2,1,0:T(8,128)} %param.8) | copy-start | bytes 24580
  3.1 0.7 %copy-start.3 = (f32[1,1,512]{2,1,0:T(1,128)S(1)}, f32[1,1,512]{2,1,0:T(1,128)}, u32[]{:S(2)}) copy-start(f32[1,1,512]{2,1,0:T(1,128)} %param.9) | copy-start | bytes 6148

commit v3 on v2

--- a/solution.py
+++ b/solution.py
@@ -12,6 +12,7 @@
 LOW = 256
 HIGH = BLK_DEV // LOW
 GROUP = 8
+UNROLL = 4
 LANES = 128
 
 F32 = jnp.float32
@@ -49,6 +50,8 @@
     acc, vec, raw, upd, srch,
     send_sem, recv_sem, kern_send, kern_recv, pair_send, pair_recv, load_sem,
 ):
+    kern_hbm, block_hbm, count_hbm, ray_hbm = (x.at[0, 0] for x in (kern_hbm, block_hbm, count_hbm, ray_hbm))
+    slope_hbm = slope_hbm.at[0]
     total = offs * wins
     part = kern_hbm.shape[1] // offs
     slots = kern_hbm.shape[2]
@@ -70,11 +73,18 @@
         return [(i, g * step_wins + i // offs, i % offs) for i in range(GROUP)]
 
     def each_group(act):
+        middle = groups // 2
+        if groups <= UNROLL:
+            for j in range(groups):
+                g = (middle + (2 * (j % 2) - 1) * ((j + 1) // 2)) % groups
+                act(g, g == 0)
+            return
+
+        @pl.loop(0, groups - 1)
+        def _(j):
+            act(middle + (2 * lax.rem(j, 2) - 1) * ((j + 1) // 2), False)
+
         act(0, True)
-
-        @pl.loop(1, groups)
-        def _(g):
-            act(g, False)
 
     loads = [
         pltpu.make_async_copy(src, dst, load_sem.at[i])
@@ -328,9 +338,7 @@
                         upd[o, h] + phi / rho * srch[o, h]
                     )
         else:
-            @pl.loop(0, groups)
-            def _(g):
-                scatter_group(g, lambda k: w_recv[step, k, :, 0:slots], beta)
+            each_group(lambda g, first: scatter_group(g, lambda k: w_recv[step, k, :, 0:slots], beta))
 
             for h in range(HIGH):
                 raw[h] = collect(h) - beta * vec[h]
@@ -366,7 +374,7 @@
             jax.ShapeDtypeStruct((cells, BLK_DEV), F32),
             jax.ShapeDtypeStruct((1, rays), F32),
         ),
-        in_specs=[pl.BlockSpec(memory_space=pl.ANY)] * 5,
+        in_specs=[pl.BlockSpec(memory_space=pltpu.HBM)] * 5,
         out_specs=(vmem, vmem),
         scratch_shapes=[
             pltpu.VMEM((wins, slots), jnp.int32),
@@ -400,9 +408,9 @@
             pltpu.SemaphoreType.DMA((5,)),
         ],
         compiler_params=pltpu.CompilerParams(
-            collective_id=0, has_side_effects=True, vmem_limit_bytes=48 * 1024 * 1024
+            collective_id=0, has_side_effects=True, vmem_limit_bytes=60 * 1024 * 1024
         ),
-    )(kernels[0, 0], blocks[0, 0], counts[0, 0], ray_of[0, 0], slopes[0])
+    )(kernels, blocks, counts, ray_of, slopes)
     return update, data[None]
 
 

time: 66 us -> 69.4 us (1.052)
  Pallas kernels: 60.6 us -> 66 us
  local copies, waits for them, and re-layouts: 4.48 us -> 2.45 us
    pallas_call x1, Pallas kernels: 60.6 us -> 66 us  [body(): pl.pallas_call(functools.partial(kernel, offs, wins), out_shape=(jax.Shap...]
    unnamed x12 -> x4, local copies, waits for them, and re-layouts: 4.48 us -> 2.45 us
where the time goes in v3:
time: 69.4 us; the launch traced here: 69.1 us
  Pallas kernels  66 us (95%)
  local copies, waits for them, and re-layouts  2.45 us (4%)
    pallas_call x1, Pallas kernels, body(): pl.pallas_call(functools.partial(kernel, offs, wins), out_shape=(jax.Shap...  66 us
    unnamed x4, local copies, waits for them, and re-layouts  2.45 us

profile of v3, /device:TPU:0, one launch (start us, length us, event | category | flops | bytes accessed | tf_op | source)
XLA Modules:
  0.0 69.1 jit_solution(3155924814802907027)
XLA Ops:
  0.6 66.0 %shard_map.68 = (f32[64,2048]{1,0:T(8,128)}, f32[1,512]{1,0:T(1,128)}) custom-call(f32[1,1,16,64,128]{4,3,2,1,0:T(8,128)} %kern_hbm.1, s32[1,1,16,128]{3,2,1,0:T(8,128)} %block_hbm.1, s32[1,1,16]{2,1,0:T(1,128)} %count_hbm.1, s32[1,1,16,128]{3,2,1,0:T(8,128)} %ray_hbm.1, f32[1,1,512]{2,1,0:T(1,128)} %slope_hbm.1), custom_call_target="tpu_custom_call" | custom-call | tf_op jit(solution)/shard_map/pallas_call | solution.py:371
  66.7 0.0 copy-start
  66.7 1.9 %copy.9 = f32[64,2048]{1,0:T(8,128)} copy(f32[64,2048]{1,0:T(8,128)} %get-tuple-element.8) | data formatting | bytes 1048576
  68.5 0.0 copy-done
  68.5 0.6 copy.10
Async XLA Ops:
  66.7 1.9 %copy-start = (f32[1,512]{1,0:T(1,128)S(1)}, f32[1,512]{1,0:T(1,128)}, u32[]{:S(2)}) copy-start(f32[1,512]{1,0:T(1,128)} %get-tuple-element.5) | copy-start | bytes 6148

commit v4 on v3

v4 whole, which is shorter than its diff:
```python
import functools

import jax
import jax.numpy as jnp
from jax import lax
from jax.experimental import pallas as pl
from jax.experimental.pallas import tpu as pltpu
from jax.sharding import PartitionSpec as P

BLK_DEV = 2048
ITERS = 3
LOW = 256
HIGH = BLK_DEV // LOW
GROUP = 8
LANES = 128

F32 = jnp.float32
BF16 = jnp.bfloat16
MESH = pl.DeviceIdType.MESH


def split2(x):
    top = x.astype(BF16)
    rest = (x - top.astype(F32)).astype(BF16)
    return top, rest


def rows_of(x):
    a = x.astype(BF16).astype(F32)
    b = (x - a).astype(BF16).astype(F32)
    c = x - a - b
    shape = (8, x.shape[1])
    i = lax.broadcasted_iota(jnp.int32, shape, 0)
    wide = lambda y: jnp.broadcast_to(y, shape)
    zero = jnp.zeros(shape, F32)
    return jnp.where(i == 0, wide(a), jnp.where(i == 1, wide(b), jnp.where(i == 2, wide(c), zero)))


def fold(x):
    return sum(x[:, i : i + LANES] for i in range(0, x.shape[1], LANES))


def kernel(
    offs, wins, kern_hbm, block_hbm, count_hbm, ray_hbm, slope_hbm,
    out_ref, data_ref,
    block_ref, count_ref, ray_ref, slope_ref,
    rays1h, ray_high, low1h, high1h, held,
    ids_send, ids_recv, w_send, w_recv, f_send, f_recv, s_send, s_recv,
    acc, model, vec, raw, upd, srch,
    ids_sem, w_sem, f_sem, kern_send, kern_recv, pair_send, pair_recv, load_sem,
):
    kern_hbm, block_hbm, count_hbm, ray_hbm = (x.at[0, 0] for x in (kern_hbm, block_hbm, count_hbm, ray_hbm))
    slope_hbm = slope_hbm.at[0]
    total = offs * wins
    part = kern_hbm.shape[1] // offs
    slots = kern_hbm.shape[2]
    ray_low = rays1h.shape[0]
    ray_parts = slope_ref.shape[1] // ray_low
    groups = total // GROUP
    width = GROUP * slots
    step_wins = GROUP // offs
    my_off = lax.axis_index("off")
    my_win = lax.axis_index("win")
    me = my_win * offs + my_off
    half = lambda o: pl.ds(pl.multiple_of(o * part, 8), part)
    off_to = [lax.rem(my_off + d, offs) for d in range(offs)]
    off_from = [lax.rem(my_off + offs - d, offs) for d in range(offs)]
    win_to = lambda d: lax.rem(my_win + d, wins)
    win_from = lambda d: lax.rem(my_win + wins - d, wins)

    def group_at(j):
        return lax.rem(groups // 2 + (2 * lax.rem(j, 2) - 1) * ((j + 1) // 2) + groups, groups)

    def each_other(act):
        @pl.loop(0, groups)
        def _(j):
            g = group_at(j)

            @pl.loop(0, step_wins)
            def _(i):
                dw = g * step_wins + i
                for do in range(offs):
                    if do == 0:
                        pl.when(dw > 0)(lambda: act(g, dw * offs, dw, 0))
                    else:
                        act(g, dw * offs + do, dw, do)

    loads = [
        pltpu.make_async_copy(src, dst, load_sem.at[i])
        for i, (src, dst) in enumerate(
            ((count_hbm, count_ref), (ray_hbm, ray_ref), (slope_hbm, slope_ref), (block_hbm, block_ref))
        )
    ]
    loads.append(pltpu.make_async_copy(kern_hbm.at[my_win, half(my_off), :], held.at[0], load_sem.at[4]))
    for load in loads:
        load.start()

    barrier = pltpu.get_barrier_semaphore()
    each_other(lambda g, k, dw, do: pl.semaphore_signal(
        barrier, inc=1, device_id=(off_to[do], win_to(dw)), device_id_type=MESH
    ))
    for load in loads:
        load.wait()

    ray_iota = lax.broadcasted_iota(jnp.int32, (ray_low, slots), 0)
    lane = lax.broadcasted_iota(jnp.int32, (1, slots), 1)
    for p in range(wins):
        ids = ray_ref[p : p + 1, :]
        high = ids // ray_low
        low = jnp.where(lane < count_ref[p], ids - high * ray_low, -1)
        rays1h[:, p * slots : (p + 1) * slots] = jnp.where(ray_iota == low, 1.0, 0.0).astype(BF16)
        ray_high[:, p * slots : (p + 1) * slots] = jnp.broadcast_to(high, (8, slots))

    def cat(pieces):
        return jnp.concatenate(pieces, axis=1)

    def take(data):
        left = jnp.concatenate(
            [rows_of(data[:, r * ray_low : (r + 1) * ray_low]) for r in range(ray_parts)], axis=0
        ).astype(BF16)
        got = jnp.dot(left, rays1h[...], preferred_element_type=F32)
        high = ray_high[...]
        picked = sum(jnp.where(high == r, got[8 * r : 8 * r + 8], 0.0) for r in range(ray_parts))
        return jnp.sum(picked, axis=0, keepdims=True)

    def gather_rays(values):
        rows = rows_of(values)
        high = ray_high[...]
        left = jnp.concatenate(
            [jnp.where(high == r, rows, 0.0) for r in range(ray_parts)], axis=0
        ).astype(BF16)
        got = lax.dot_general(left, rays1h[...], (((1,), (1,)), ((), ())), preferred_element_type=F32)
        return cat([jnp.sum(got[8 * r : 8 * r + 8], axis=0, keepdims=True) for r in range(ray_parts)])

    def total_of(partials):
        return jnp.sum(jnp.sum(partials, axis=0), axis=1, keepdims=True)

    def bytes_in(ref, sem):
        pltpu.make_async_copy(ref, ref, sem).wait()

    for p in range(wins):
        ids = block_ref[p : p + 1, :]
        high = ids // LOW
        ids_send[p, :, 0:slots] = (ids - high * LOW).astype(F32)
        ids_send[p, :, slots : 2 * slots] = high.astype(F32)
    ids_recv[0] = ids_send[my_win]
    vec[...] = jnp.zeros_like(vec)
    srch[my_off] = jnp.zeros_like(vec)
    upd[my_off] = jnp.zeros_like(vec)
    raw[...] = jnp.zeros_like(raw)

    pl.semaphore_wait(barrier, total - 1)

    def to_owner(source_of, target_of, s_sem, r_sem_of):
        def send(g, k, dw, do):
            win = win_to(dw)
            pltpu.make_async_remote_copy(
                src_ref=source_of(win, do), dst_ref=target_of(k),
                send_sem=s_sem, recv_sem=r_sem_of(g),
                device_id=(off_to[do], win), device_id_type=MESH,
            ).start()

        each_other(send)

    to_owner(lambda win, do: ids_send.at[win], lambda k: ids_recv.at[k], ids_sem.at[0], lambda g: ids_sem.at[1])

    def kern_of(g):
        return cat([held[g * GROUP + i] for i in range(GROUP)])

    low_iota = lax.broadcasted_iota(jnp.int32, (LOW, slots), 0).astype(F32)

    def build_one_hots():
        bytes_in(ids_recv.at[pl.ds(1, total - 1)], ids_sem.at[1])

        @pl.loop(0, groups)
        def _(g):
            for i in range(GROUP):
                here = pl.ds(i * slots, slots)
                low = ids_recv[g * GROUP + i, :, 0:slots]
                low1h[g, :, here] = jnp.where(low_iota == low, 1.0, 0.0).astype(BF16)
                high = jnp.broadcast_to(ids_recv[g * GROUP + i, :, slots : 2 * slots], (16, slots))
                for h in range(HIGH):
                    high1h[g, h, :, here] = jnp.where(high == h, 1.0, 0.0).astype(BF16)

    def one_step(step, carry):
        data, alpha, rho, rhobar, phibar, sine, cosine = carry
        first = step == 0
        weights = take(data)
        partial = fold(data * data)
        for p in range(wins):
            w_send[step, p, :, 0:slots] = weights[:, p * slots : (p + 1) * slots]
            w_send[step, p, :, slots : 2 * slots] = partial
        to_owner(
            lambda win, do: w_send.at[step, win], lambda k: w_recv.at[step, k],
            w_sem.at[0, step], lambda g: w_sem.at[1, step],
        )

        @pl.when(first)
        def _():
            to_owner(
                lambda win, do: kern_hbm.at[win, half(off_to[do]), :], lambda k: held.at[k],
                kern_send, lambda g: kern_recv.at[g],
            )
            build_one_hots()

        theta_rho = sine * alpha / rho
        for h in range(HIGH):
            fresh = raw[h] / alpha
            vec[h] = fresh
            srch[my_off, h] = fresh - theta_rho * srch[my_off, h]
        acc[...] = jnp.zeros_like(acc)

        w_recv[step, 0] = w_send[step, my_win]
        bytes_in(w_recv.at[step, pl.ds(1, total - 1)], w_sem.at[1, step])
        beta = jnp.sqrt(total_of(w_recv[step, :, :, slots : 2 * slots]))
        data = data / beta
        rho = jnp.sqrt(rhobar * rhobar + beta * beta)
        cosine = rhobar / rho
        sine = beta / rho
        phi = cosine * phibar
        phibar = jnp.where(first, beta, sine * phibar)

        @pl.loop(0, groups)
        def _(j):
            g = group_at(j)

            @pl.when(first)
            def _():
                @pl.when(g > 0)
                def _():
                    bytes_in(held.at[pl.ds(g * GROUP, GROUP)], kern_recv.at[g])

                @pl.when(g == 0)
                def _():
                    bytes_in(held.at[pl.ds(1, GROUP - 1)], kern_recv.at[0])

            row = cat([w_recv[step, g * GROUP + i, :, 0:slots] for i in range(GROUP)]) / beta
            parts = split2(kern_of(g) * row)
            rows = []
            for h in range(HIGH):
                mask = jnp.concatenate([high1h[g, h]] * (part // 16), axis=0)
                rows.append(cat([piece * mask for piece in parts]))
            left = jnp.concatenate(rows, axis=0)
            low = low1h[g]
            acc[...] += lax.dot_general(
                left, cat([low, low]), (((1,), (1,)), ((), ())), preferred_element_type=F32
            )

        square = jnp.zeros((part, LOW), F32)
        for h in range(HIGH):
            piece = acc[h * part : (h + 1) * part, :] - beta * vec[h]
            raw[h] = piece
            square += piece * piece
            for c, half_piece in enumerate(split2(piece)):
                model[h * part : (h + 1) * part, c * LOW : (c + 1) * LOW] = half_piece
            upd[my_off, h] = upd[my_off, h] + phi / rho * srch[my_off, h]
        norm = fold(jnp.sum(square, axis=0, keepdims=True))

        @pl.loop(0, groups)
        def _(j):
            g = group_at(j)
            low = low1h[g]
            got = jnp.dot(model[...], jnp.concatenate([low, low], axis=0), preferred_element_type=F32)
            high = jnp.broadcast_to(
                cat([ids_recv[g * GROUP + i, :, slots : 2 * slots] for i in range(GROUP)]), (8, width)
            )
            fetched = [jnp.zeros((8, width), F32)] * (part // 8)
            for h in range(HIGH):
                hit = high == h
                for r in range(part // 8):
                    at = h * part + r * 8
                    fetched[r] = jnp.where(hit, got[at : at + 8], fetched[r])
            rows = kern_of(g)
            mixed = sum(fetched[r] * rows[r * 8 : r * 8 + 8] for r in range(part // 8))
            values = jnp.sum(mixed, axis=0, keepdims=True)
            for i in range(GROUP):
                k = g * GROUP + i
                f_send[step, k, :, 0:slots] = values[:, i * slots : (i + 1) * slots]
                f_send[step, k, :, slots : 2 * slots] = norm

            @pl.loop(0, step_wins)
            def _(i):
                dw = g * step_wins + i

                def send(do):
                    k = dw * offs + do
                    pltpu.make_async_remote_copy(
                        src_ref=f_send.at[step, k], dst_ref=f_recv.at[step, me],
                        send_sem=f_sem.at[0, step], recv_sem=f_sem.at[1, step],
                        device_id=(off_from[do], win_from(dw)), device_id_type=MESH,
                    ).start()

                pl.when(dw > 0)(lambda: send(0))
                for do in range(1, offs):
                    send(do)

        f_recv[step, me] = f_send[step, 0]
        bytes_in(f_recv.at[step, pl.ds(1, total - 1)], f_sem.at[1, step])
        alpha = jnp.sqrt(total_of(f_recv[step, :, :, slots : 2 * slots]))
        terms = cat([
            sum(f_recv[step, p * offs + o, :, 0:slots] for o in range(offs)) for p in range(wins)
        ])
        data = gather_rays(terms) / alpha - alpha * data
        rhobar = jnp.where(first, alpha, -cosine * alpha)
        sine = jnp.where(first, jnp.zeros_like(sine), sine)
        return data, alpha, rho, rhobar, phibar, sine, cosine

    one = jnp.ones((1, 1), F32)
    zero = jnp.zeros((1, 1), F32)
    data, alpha, rho, rhobar, phibar, sine, cosine = lax.fori_loop(
        0, ITERS, one_step, (slope_ref[...], one, one, zero, zero, zero, zero)
    )

    s_send[...] = fold(data * data)
    to_owner(lambda win, do: s_send, lambda k: s_recv.at[k], w_sem.at[0, ITERS], lambda g: w_sem.at[1, ITERS])
    theta_rho = sine * alpha / rho
    for h in range(HIGH):
        srch[my_off, h] = raw[h] / alpha - theta_rho * srch[my_off, h]
    for other in range(1, offs):
        for which, ref in enumerate((upd, srch)):
            pltpu.make_async_remote_copy(
                src_ref=ref.at[my_off], dst_ref=ref.at[my_off],
                send_sem=pair_send.at[which, other], recv_sem=pair_recv.at[which, other],
                device_id=(off_to[other], my_win), device_id_type=MESH,
            ).start()
    s_recv[0] = s_send[...]
    bytes_in(s_recv.at[pl.ds(1, total - 1)], w_sem.at[1, ITERS])
    beta = jnp.sqrt(total_of(s_recv[...]))
    data_ref[...] = data / beta
    rho = jnp.sqrt(rhobar * rhobar + beta * beta)
    phi = rhobar / rho * phibar
    for other in range(1, offs):
        for which, ref in enumerate((upd, srch)):
            bytes_in(ref.at[0], pair_recv.at[which, other])
    for o in range(offs):
        for h in range(HIGH):
            out_ref[o * part : (o + 1) * part, h * LOW : (h + 1) * LOW] = (
                upd[o, h] + phi / rho * srch[o, h]
            )

    bytes_in(ids_recv.at[pl.ds(1, total - 1)], ids_sem.at[0])
    bytes_in(held.at[pl.ds(1, total - 1)], kern_send)
    for step in range(ITERS):
        bytes_in(f_recv.at[step, pl.ds(1, total - 1)], f_sem.at[0, step])
        bytes_in(w_recv.at[step, pl.ds(1, total - 1)], w_sem.at[0, step])
    bytes_in(s_recv.at[pl.ds(1, total - 1)], w_sem.at[0, ITERS])
    for other in range(1, offs):
        for which, ref in enumerate((upd, srch)):
            bytes_in(ref.at[0], pair_send.at[which, other])


def body(kernels, blocks, counts, ray_of, slopes):
    offs, wins = lax.axis_size("off"), lax.axis_size("win")
    total = offs * wins
    cells, slots = kernels.shape[3:]
    rays = slopes.shape[2]
    part = cells // offs
    groups = total // GROUP
    ray_low = LOW if rays % LOW == 0 else rays
    vmem = pl.BlockSpec(memory_space=pltpu.VMEM)
    model = (HIGH, part, LOW)
    update, data = pl.pallas_call(
        functools.partial(kernel, offs, wins),
        out_shape=(
            jax.ShapeDtypeStruct((cells, BLK_DEV), F32),
            jax.ShapeDtypeStruct((1, rays), F32),
        ),
        in_specs=[pl.BlockSpec(memory_space=pltpu.HBM)] * 5,
        out_specs=(vmem, vmem),
        scratch_shapes=[
            pltpu.VMEM((wins, slots), jnp.int32),
            pltpu.SMEM((wins,), jnp.int32),
            pltpu.VMEM((wins, slots), jnp.int32),
            pltpu.VMEM((1, rays), F32),
            pltpu.VMEM((ray_low, wins * slots), BF16),
            pltpu.VMEM((8, wins * slots), jnp.int32),
            pltpu.VMEM((groups, LOW, GROUP * slots), BF16),
            pltpu.VMEM((groups, HIGH, 16, GROUP * slots), BF16),
            pltpu.VMEM((total, part, slots), F32),
            pltpu.VMEM((wins, 1, 2 * slots), F32),
            pltpu.VMEM((total, 1, 2 * slots), F32),
            pltpu.VMEM((ITERS, wins, 1, 2 * slots), F32),
            pltpu.VMEM((ITERS, total, 1, 2 * slots), F32),
            pltpu.VMEM((ITERS, total, 1, 2 * slots), F32),
            pltpu.VMEM((ITERS, total, 1, 2 * slots), F32),
            pltpu.VMEM((1, slots), F32),
            pltpu.VMEM((total, 1, slots), F32),
            pltpu.VMEM((HIGH * part, LOW), F32),
            pltpu.VMEM((HIGH * part, 2 * LOW), BF16),
            pltpu.VMEM(model, F32),
            pltpu.VMEM(model, F32),
            pltpu.VMEM((offs,) + model, F32),
            pltpu.VMEM((offs,) + model, F32),
            pltpu.SemaphoreType.DMA((2,)),
            pltpu.SemaphoreType.DMA((2, ITERS + 1)),
            pltpu.SemaphoreType.DMA((2, ITERS)),
            pltpu.SemaphoreType.DMA,
            pltpu.SemaphoreType.DMA((groups,)),
            pltpu.SemaphoreType.DMA((2, offs)),
            pltpu.SemaphoreType.DMA((2, offs)),
            pltpu.SemaphoreType.DMA((5,)),
        ],
        compiler_params=pltpu.CompilerParams(
            collective_id=0, has_side_effects=True, vmem_limit_bytes=60 * 1024 * 1024
        ),
    )(kernels, blocks, counts, ray_of, slopes)
    return update, data[None]


def solution(mesh):
    in_specs = (
        P("off", "win", None, None, None),
        P("off", "win", None, None),
        P("off", "win", None),
        P("off", "win", None, None),
        P("off", "win", None),
    )
    out_specs = (P(None, "win"), P("off", "win", None))
    return jax.shard_map(body, mesh=mesh, in_specs=in_specs, out_specs=out_specs, check_vma=False)
```

time: 69.4 us -> 67.2 us (0.968)
  Pallas kernels: 66 us -> 63.9 us
    pallas_call x1, Pallas kernels: 66 us -> 63.9 us  [body(): pl.pallas_call(functools.partial(kernel, offs, wins), out_shape=(jax.Shap...]
where the time goes in v4:
time: 67.2 us; the launch traced here: 67 us
  Pallas kernels  63.9 us (95%)
  local copies, waits for them, and re-layouts  2.45 us (4%)
    pallas_call x1, Pallas kernels, body(): pl.pallas_call(functools.partial(kernel, offs, wins), out_shape=(jax.Shap...  63.9 us
    unnamed x4, local copies, waits for them, and re-layouts  2.45 us

profile of v4, /device:TPU:0, one launch (start us, length us, event | category | flops | bytes accessed | tf_op | source)
XLA Modules:
  0.0 67.0 jit_solution(7800479086521005422)
XLA Ops:
  0.6 63.9 %shard_map.68 = (f32[64,2048]{1,0:T(8,128)}, f32[1,512]{1,0:T(1,128)}) custom-call(f32[1,1,16,64,128]{4,3,2,1,0:T(8,128)} %kern_hbm.1, s32[1,1,16,128]{3,2,1,0:T(8,128)} %block_hbm.1, s32[1,1,16]{2,1,0:T(1,128)} %count_hbm.1, s32[1,1,16,128]{3,2,1,0:T(8,128)} %ray_hbm.1, f32[1,1,512]{2,1,0:T(1,128)} %slope_hbm.1), custom_call_target="tpu_custom_call" | custom-call | tf_op jit(solution)/shard_map/pallas_call | solution.py:362
  64.5 0.0 copy-start
  64.5 1.9 %copy.9 = f32[64,2048]{1,0:T(8,128)} copy(f32[64,2048]{1,0:T(8,128)} %get-tuple-element.8) | data formatting | bytes 1048576
  66.4 0.0 copy-done
  66.4 0.6 copy.10
Async XLA Ops:
  64.5 1.9 %copy-start = (f32[1,512]{1,0:T(1,128)S(1)}, f32[1,512]{1,0:T(1,128)}, u32[]{:S(2)}) copy-start(f32[1,512]{1,0:T(1,128)} %get-tuple-element.5) | copy-start | bytes 6148

commit v5 on v4

v5 whole, which is shorter than its diff:
```python
import functools

import jax
import jax.numpy as jnp
from jax import lax
from jax.experimental import pallas as pl
from jax.experimental.pallas import tpu as pltpu
from jax.sharding import PartitionSpec as P

BLK_DEV = 2048
ITERS = 3
LOW = 256
HIGH = BLK_DEV // LOW
GROUP = 8
LANES = 128

F32 = jnp.float32
BF16 = jnp.bfloat16
MESH = pl.DeviceIdType.MESH


def split2(x):
    top = x.astype(BF16)
    rest = (x - top.astype(F32)).astype(BF16)
    return top, rest


def rows_of(x):
    a = x.astype(BF16).astype(F32)
    b = (x - a).astype(BF16).astype(F32)
    c = x - a - b
    shape = (8, x.shape[1])
    i = lax.broadcasted_iota(jnp.int32, shape, 0)
    wide = lambda y: jnp.broadcast_to(y, shape)
    zero = jnp.zeros(shape, F32)
    return jnp.where(i == 0, wide(a), jnp.where(i == 1, wide(b), jnp.where(i == 2, wide(c), zero)))


def fold(x):
    return sum(x[:, i : i + LANES] for i in range(0, x.shape[1], LANES))


def kernel(
    offs, wins, kern_hbm, block_hbm, count_hbm, ray_hbm, slope_hbm,
    out_ref, data_ref,
    block_ref, count_ref, ray_ref, slope_ref,
    rays1h, ray_high, low1h, high1h, arrived, held,
    ids_send, ids_recv, w_send, w_recv, f_send, f_swap, f_recv, s_send, s_recv, s_sum,
    acc, model, vec, raw, upd, srch,
    ids_sem, ids_pair, w_sem, w_pair, f_sem, f_pair, s_pair, kern_pair, kern_send, kern_recv, pair_send, pair_recv, load_sem,
):
    kern_hbm, block_hbm, count_hbm, ray_hbm = (x.at[0, 0] for x in (kern_hbm, block_hbm, count_hbm, ray_hbm))
    slope_hbm = slope_hbm.at[0]
    total = offs * wins
    part = kern_hbm.shape[1] // offs
    slots = kern_hbm.shape[2]
    ray_low = rays1h.shape[0]
    ray_parts = slope_ref.shape[1] // ray_low
    groups = total // GROUP
    width = GROUP * slots
    class_groups = wins // GROUP
    my_off = lax.axis_index("off")
    my_win = lax.axis_index("win")
    me = my_win * offs + my_off
    half = lambda o: pl.ds(pl.multiple_of(o * part, 8), part)
    off_to = [lax.rem(my_off + d, offs) for d in range(offs)]
    off_from = [lax.rem(my_off + offs - d, offs) for d in range(offs)]
    win_to = lambda d: lax.rem(my_win + d, wins)
    win_from = lambda d: lax.rem(my_win + wins - d, wins)

    def each_win(act):
        @pl.loop(1, wins)
        def _(d):
            act(d, win_to(d), win_from(d))

    def each_core(act):
        for c in range(1, offs):
            act(c, off_to[c], off_from[c])

    def remote(src, dst, s_sem, r_sem, core, win):
        pltpu.make_async_remote_copy(
            src_ref=src, dst_ref=dst, send_sem=s_sem, recv_sem=r_sem,
            device_id=(core, win), device_id_type=MESH,
        ).start()

    loads = [
        pltpu.make_async_copy(src, dst, load_sem.at[i])
        for i, (src, dst) in enumerate(
            ((count_hbm, count_ref), (ray_hbm, ray_ref), (slope_hbm, slope_ref), (block_hbm, block_ref))
        )
    ]
    loads.append(pltpu.make_async_copy(kern_hbm.at[my_win], arrived.at[0], load_sem.at[4]))
    for load in loads:
        load.start()

    barrier = pltpu.get_barrier_semaphore()
    greet = lambda core, win: pl.semaphore_signal(
        barrier, inc=1, device_id=(core, win), device_id_type=MESH
    )
    each_win(lambda d, to, _: greet(my_off, to))
    each_core(lambda c, to, _: greet(to, my_win))
    for load in loads:
        load.wait()

    ray_iota = lax.broadcasted_iota(jnp.int32, (ray_low, slots), 0)
    lane = lax.broadcasted_iota(jnp.int32, (1, slots), 1)
    for p in range(wins):
        ids = ray_ref[p : p + 1, :]
        high = ids // ray_low
        low = jnp.where(lane < count_ref[p], ids - high * ray_low, -1)
        rays1h[:, p * slots : (p + 1) * slots] = jnp.where(ray_iota == low, 1.0, 0.0).astype(BF16)
        ray_high[:, p * slots : (p + 1) * slots] = jnp.broadcast_to(high, (8, slots))

    def cat(pieces):
        return jnp.concatenate(pieces, axis=1)

    def take(data):
        left = jnp.concatenate(
            [rows_of(data[:, r * ray_low : (r + 1) * ray_low]) for r in range(ray_parts)], axis=0
        ).astype(BF16)
        got = jnp.dot(left, rays1h[...], preferred_element_type=F32)
        high = ray_high[...]
        picked = sum(jnp.where(high == r, got[8 * r : 8 * r + 8], 0.0) for r in range(ray_parts))
        return jnp.sum(picked, axis=0, keepdims=True)

    def gather_rays(values):
        rows = rows_of(values)
        high = ray_high[...]
        left = jnp.concatenate(
            [jnp.where(high == r, rows, 0.0) for r in range(ray_parts)], axis=0
        ).astype(BF16)
        got = lax.dot_general(left, rays1h[...], (((1,), (1,)), ((), ())), preferred_element_type=F32)
        return cat([jnp.sum(got[8 * r : 8 * r + 8], axis=0, keepdims=True) for r in range(ray_parts)])

    def total_of(partials):
        return jnp.sum(jnp.sum(partials, axis=0), axis=1, keepdims=True)

    def bytes_in(ref, sem):
        pltpu.make_async_copy(ref, ref, sem).wait()

    for p in range(wins):
        ids = block_ref[p : p + 1, :]
        high = ids // LOW
        ids_send[p, :, 0:slots] = (ids - high * LOW).astype(F32)
        ids_send[p, :, slots : 2 * slots] = high.astype(F32)
    ids_recv[0, 0] = ids_send[my_win]
    vec[...] = jnp.zeros_like(vec)
    srch[my_off] = jnp.zeros_like(vec)
    upd[my_off] = jnp.zeros_like(vec)
    raw[...] = jnp.zeros_like(raw)

    pl.semaphore_wait(barrier, wins - 1 + offs - 1)

    def to_owner(source_of, box, s_sem, r_sem):
        each_win(lambda d, to, _: remote(source_of(to), box.at[0, d], s_sem, r_sem, my_off, to))

    def swap(box, sems):
        each_core(lambda c, _, back: remote(box.at[0], box.at[c], sems.at[0, c], sems.at[1, c], back, my_win))

    def swapped(box, sems, side):
        for c in range(1, offs):
            bytes_in(box.at[c], sems.at[side, c])

    to_owner(lambda win: ids_send.at[win], ids_recv, ids_sem.at[0], ids_sem.at[1])

    def kern_of(k):
        return cat([held[k + i] for i in range(GROUP)])

    def pieces_of(box, k, begin):
        c, d = k // wins, lax.rem(k, wins)
        return cat([box[c, d + i, :, begin : begin + slots] for i in range(GROUP)])

    low_iota = lax.broadcasted_iota(jnp.int32, (LOW, width), 0).astype(F32)

    def build_one_hots():
        bytes_in(ids_recv.at[0, pl.ds(1, wins - 1)], ids_sem.at[1])
        swap(ids_recv, ids_pair)
        swapped(ids_recv, ids_pair, 1)

        @pl.loop(0, groups)
        def _(g):
            low = pieces_of(ids_recv, g * GROUP, 0)
            high = jnp.broadcast_to(pieces_of(ids_recv, g * GROUP, slots), (16, width))
            low1h[g] = jnp.where(low_iota == low, 1.0, 0.0).astype(BF16)
            for h in range(HIGH):
                high1h[g, h] = jnp.where(high == h, 1.0, 0.0).astype(BF16)

    def one_step(step, carry):
        data, alpha, rho, rhobar, phibar, sine, cosine = carry
        first = step == 0
        weights = take(data)
        partial = fold(data * data)
        for p in range(wins):
            w_send[step, p, :, 0:slots] = weights[:, p * slots : (p + 1) * slots]
            w_send[step, p, :, slots : 2 * slots] = partial
        to_owner(lambda win: w_send.at[step, win], w_recv.at[step], w_sem.at[0, step], w_sem.at[1, step])

        @pl.when(first)
        def _():
            each_win(lambda d, to, _: remote(
                kern_hbm.at[to], arrived.at[d], kern_send, kern_recv.at[d // GROUP], my_off, to
            ))
            build_one_hots()

        theta_rho = sine * alpha / rho
        for h in range(HIGH):
            fresh = raw[h] / alpha
            vec[h] = fresh
            srch[my_off, h] = fresh - theta_rho * srch[my_off, h]
        acc[...] = jnp.zeros_like(acc)

        w_recv[step, 0, 0] = w_send[step, my_win]
        bytes_in(w_recv.at[step, 0, pl.ds(1, wins - 1)], w_sem.at[1, step])
        swap(w_recv.at[step], w_pair.at[step])

        @pl.loop(0, groups)
        def _(g):
            k = g * GROUP

            @pl.when(first & (g < class_groups))
            def _():
                pl.when(g == 0)(lambda: bytes_in(arrived.at[pl.ds(1, GROUP - 1)], kern_recv.at[0]))
                pl.when(g > 0)(lambda: bytes_in(arrived.at[pl.ds(k, GROUP)], kern_recv.at[g]))
                for c in range(1, offs):
                    remote(
                        arrived.at[pl.ds(k, GROUP), half(off_from[c]), :],
                        held.at[pl.ds(c * wins + k, GROUP)],
                        kern_pair.at[0, c], kern_pair.at[1, c * class_groups + g], off_from[c], my_win,
                    )
                for i in range(GROUP):
                    held[k + i] = arrived[k + i, half(my_off), :]

            @pl.when(first & (g >= class_groups))
            def _():
                bytes_in(held.at[pl.ds(k, GROUP)], kern_pair.at[1, g])

            @pl.when(g == class_groups)
            def _():
                swapped(w_recv.at[step], w_pair.at[step], 1)

            row = pieces_of(w_recv.at[step], k, 0)
            parts = split2(kern_of(k) * row)
            rows = []
            for h in range(HIGH):
                mask = jnp.concatenate([high1h[g, h]] * (part // 16), axis=0)
                rows.append(cat([piece * mask for piece in parts]))
            left = jnp.concatenate(rows, axis=0)
            low = low1h[g]
            acc[...] += lax.dot_general(
                left, cat([low, low]), (((1,), (1,)), ((), ())), preferred_element_type=F32
            )

        norms = w_recv[step, :, :, :, slots : 2 * slots].reshape(total, 1, slots)
        beta = jnp.sqrt(total_of(norms))
        data = data / beta
        rho = jnp.sqrt(rhobar * rhobar + beta * beta)
        cosine = rhobar / rho
        sine = beta / rho
        phi = cosine * phibar
        phibar = jnp.where(first, beta, sine * phibar)

        square = jnp.zeros((part, LOW), F32)
        for h in range(HIGH):
            piece = acc[h * part : (h + 1) * part, :] / beta - beta * vec[h]
            raw[h] = piece
            square += piece * piece
            for c, half_piece in enumerate(split2(piece)):
                model[h * part : (h + 1) * part, c * LOW : (c + 1) * LOW] = half_piece
            upd[my_off, h] = upd[my_off, h] + phi / rho * srch[my_off, h]
        norm = fold(jnp.sum(square, axis=0, keepdims=True))

        @pl.loop(0, groups)
        def _(j):
            g = groups - 1 - j
            k = g * GROUP
            low = low1h[g]
            got = jnp.dot(model[...], jnp.concatenate([low, low], axis=0), preferred_element_type=F32)
            high = jnp.broadcast_to(pieces_of(ids_recv, k, slots), (8, width))
            fetched = [jnp.zeros((8, width), F32)] * (part // 8)
            for h in range(HIGH):
                hit = high == h
                for r in range(part // 8):
                    at = h * part + r * 8
                    fetched[r] = jnp.where(hit, got[at : at + 8], fetched[r])
            rows = kern_of(k)
            mixed = sum(fetched[r] * rows[r * 8 : r * 8 + 8] for r in range(part // 8))
            values = jnp.sum(mixed, axis=0, keepdims=True)
            c, d = k // wins, lax.rem(k, wins)
            for i in range(GROUP):
                f_send[step, c, d + i, :, 0:slots] = values[:, i * slots : (i + 1) * slots]
                f_send[step, c, d + i, :, slots : 2 * slots] = norm

            @pl.when(g == class_groups)
            def _():
                each_core(lambda c, to, _: remote(
                    f_send.at[step, c], f_swap.at[step, c], f_pair.at[0, step, c], f_pair.at[1, step, c],
                    to, my_win,
                ))

        for c in range(1, offs):
            bytes_in(f_swap.at[step, c], f_pair.at[1, step, c])
        f_send[step, 0] = f_send[step, 0] + sum(f_swap[step, c] for c in range(1, offs))
        each_win(lambda d, _, back: remote(
            f_send.at[step, 0, d], f_recv.at[step, my_win], f_sem.at[0, step], f_sem.at[1, step], my_off, back
        ))
        f_recv[step, my_win] = f_send[step, 0, 0]
        bytes_in(f_recv.at[step, pl.ds(1, wins - 1)], f_sem.at[1, step])
        alpha = jnp.sqrt(total_of(f_recv[step, :, :, slots : 2 * slots]))
        terms = cat([f_recv[step, p, :, 0:slots] for p in range(wins)])
        data = gather_rays(terms) / alpha - alpha * data
        rhobar = jnp.where(first, alpha, -cosine * alpha)
        sine = jnp.where(first, jnp.zeros_like(sine), sine)
        return data, alpha, rho, rhobar, phibar, sine, cosine

    one = jnp.ones((1, 1), F32)
    zero = jnp.zeros((1, 1), F32)
    data, alpha, rho, rhobar, phibar, sine, cosine = lax.fori_loop(
        0, ITERS, one_step, (slope_ref[...], one, one, zero, zero, zero, zero)
    )

    s_send[...] = fold(data * data)
    s_recv[0, 0] = s_send[...]
    to_owner(lambda win: s_send, s_recv, w_sem.at[0, ITERS], w_sem.at[1, ITERS])
    theta_rho = sine * alpha / rho
    for h in range(HIGH):
        srch[my_off, h] = raw[h] / alpha - theta_rho * srch[my_off, h]
    for other in range(1, offs):
        for which, ref in enumerate((upd, srch)):
            pltpu.make_async_remote_copy(
                src_ref=ref.at[my_off], dst_ref=ref.at[my_off],
                send_sem=pair_send.at[which, other], recv_sem=pair_recv.at[which, other],
                device_id=(off_to[other], my_win), device_id_type=MESH,
            ).start()
    bytes_in(s_recv.at[0, pl.ds(1, wins - 1)], w_sem.at[1, ITERS])
    s_sum[0] = jnp.sum(s_recv[0], axis=0)
    swap(s_sum, s_pair)
    swapped(s_sum, s_pair, 1)
    beta = jnp.sqrt(total_of(s_sum[...]))
    data_ref[...] = data / beta
    rho = jnp.sqrt(rhobar * rhobar + beta * beta)
    phi = rhobar / rho * phibar
    for other in range(1, offs):
        for which, ref in enumerate((upd, srch)):
            bytes_in(ref.at[0], pair_recv.at[which, other])
    for o in range(offs):
        for h in range(HIGH):
            out_ref[o * part : (o + 1) * part, h * LOW : (h + 1) * LOW] = (
                upd[o, h] + phi / rho * srch[o, h]
            )

    others = pl.ds(1, wins - 1)
    bytes_in(ids_recv.at[0, others], ids_sem.at[0])
    swapped(ids_recv, ids_pair, 0)
    bytes_in(arrived.at[others], kern_send)
    for c in range(1, offs):
        bytes_in(held.at[pl.ds(0, wins)], kern_pair.at[0, c])
    for step in range(ITERS):
        bytes_in(f_recv.at[step, others], f_sem.at[0, step])
        bytes_in(w_recv.at[step, 0, others], w_sem.at[0, step])
        swapped(w_recv.at[step], w_pair.at[step], 0)
        for c in range(1, offs):
            bytes_in(f_swap.at[step, c], f_pair.at[0, step, c])
    bytes_in(s_recv.at[0, others], w_sem.at[0, ITERS])
    swapped(s_sum, s_pair, 0)
    for other in range(1, offs):
        for which, ref in enumerate((upd, srch)):
            bytes_in(ref.at[0], pair_send.at[which, other])


def body(kernels, blocks, counts, ray_of, slopes):
    offs, wins = lax.axis_size("off"), lax.axis_size("win")
    total = offs * wins
    cells, slots = kernels.shape[3:]
    rays = slopes.shape[2]
    part = cells // offs
    groups = total // GROUP
    ray_low = LOW if rays % LOW == 0 else rays
    vmem = pl.BlockSpec(memory_space=pltpu.VMEM)
    model = (HIGH, part, LOW)
    update, data = pl.pallas_call(
        functools.partial(kernel, offs, wins),
        out_shape=(
            jax.ShapeDtypeStruct((cells, BLK_DEV), F32),
            jax.ShapeDtypeStruct((1, rays), F32),
        ),
        in_specs=[pl.BlockSpec(memory_space=pltpu.HBM)] * 5,
        out_specs=(vmem, vmem),
        scratch_shapes=[
            pltpu.VMEM((wins, slots), jnp.int32),
            pltpu.SMEM((wins,), jnp.int32),
            pltpu.VMEM((wins, slots), jnp.int32),
            pltpu.VMEM((1, rays), F32),
            pltpu.VMEM((ray_low, wins * slots), BF16),
            pltpu.VMEM((8, wins * slots), jnp.int32),
            pltpu.VMEM((groups, LOW, GROUP * slots), BF16),
            pltpu.VMEM((groups, HIGH, 16, GROUP * slots), BF16),
            pltpu.VMEM((wins, cells, slots), F32),
            pltpu.VMEM((total, part, slots), F32),
            pltpu.VMEM((wins, 1, 2 * slots), F32),
            pltpu.VMEM((offs, wins, 1, 2 * slots), F32),
            pltpu.VMEM((ITERS, wins, 1, 2 * slots), F32),
            pltpu.VMEM((ITERS, offs, wins, 1, 2 * slots), F32),
            pltpu.VMEM((ITERS, offs, wins, 1, 2 * slots), F32),
            pltpu.VMEM((ITERS, offs, wins, 1, 2 * slots), F32),
            pltpu.VMEM((ITERS, wins, 1, 2 * slots), F32),
            pltpu.VMEM((1, slots), F32),
            pltpu.VMEM((1, wins, 1, slots), F32),
            pltpu.VMEM((offs, 1, slots), F32),
            pltpu.VMEM((HIGH * part, LOW), F32),
            pltpu.VMEM((HIGH * part, 2 * LOW), BF16),
            pltpu.VMEM(model, F32),
            pltpu.VMEM(model, F32),
            pltpu.VMEM((offs,) + model, F32),
            pltpu.VMEM((offs,) + model, F32),
            pltpu.SemaphoreType.DMA((2,)),
            pltpu.SemaphoreType.DMA((2, offs)),
            pltpu.SemaphoreType.DMA((2, ITERS + 1)),
            pltpu.SemaphoreType.DMA((ITERS, 2, offs)),
            pltpu.SemaphoreType.DMA((2, ITERS)),
            pltpu.SemaphoreType.DMA((2, ITERS, offs)),
            pltpu.SemaphoreType.DMA((2, offs)),
            pltpu.SemaphoreType.DMA((2, groups)),
            pltpu.SemaphoreType.DMA,
            pltpu.SemaphoreType.DMA((groups,)),
            pltpu.SemaphoreType.DMA((2, offs)),
            pltpu.SemaphoreType.DMA((2, offs)),
            pltpu.SemaphoreType.DMA((5,)),
        ],
        compiler_params=pltpu.CompilerParams(
            collective_id=0, has_side_effects=True, vmem_limit_bytes=60 * 1024 * 1024
        ),
    )(kernels, blocks, counts, ray_of, slopes)
    return update, data[None]


def solution(mesh):
    in_specs = (
        P("off", "win", None, None, None),
        P("off", "win", None, None),
        P("off", "win", None),
        P("off", "win", None, None),
        P("off", "win", None),
    )
    out_specs = (P(None, "win"), P("off", "win", None))
    return jax.shard_map(body, mesh=mesh, in_specs=in_specs, out_specs=out_specs, check_vma=False)
```

time: 67.2 us -> 65.9 us (0.981)
  Pallas kernels: 63.9 us -> 62.6 us
    pallas_call x1, Pallas kernels: 63.9 us -> 62.6 us  [body(): pl.pallas_call(functools.partial(kernel, offs, wins), out_shape=(jax.Shap...]
where the time goes in v5:
time: 65.9 us; the launch traced here: 65.7 us
  Pallas kernels  62.6 us (95%)
  local copies, waits for them, and re-layouts  2.45 us (4%)
    pallas_call x1, Pallas kernels, body(): pl.pallas_call(functools.partial(kernel, offs, wins), out_shape=(jax.Shap...  62.6 us
    unnamed x4, local copies, waits for them, and re-layouts  2.45 us

profile of v5, /device:TPU:0, one launch (start us, length us, event | category | flops | bytes accessed | tf_op | source)
XLA Modules:
  0.0 65.7 jit_solution(4094108139778724770)
XLA Ops:
  0.6 62.6 %shard_map.68 = (f32[64,2048]{1,0:T(8,128)}, f32[1,512]{1,0:T(1,128)}) custom-call(f32[1,1,16,64,128]{4,3,2,1,0:T(8,128)} %kern_hbm.1, s32[1,1,16,128]{3,2,1,0:T(8,128)} %block_hbm.1, s32[1,1,16]{2,1,0:T(1,128)} %count_hbm.1, s32[1,1,16,128]{3,2,1,0:T(8,128)} %ray_hbm.1, f32[1,1,512]{2,1,0:T(1,128)} %slope_hbm.1), custom_call_target="tpu_custom_call" | custom-call | tf_op jit(solution)/shard_map/pallas_call | solution.py:380
  63.2 0.0 copy-start
  63.2 1.9 %copy.9 = f32[64,2048]{1,0:T(8,128)} copy(f32[64,2048]{1,0:T(8,128)} %get-tuple-element.8) | data formatting | bytes 1048576
  65.1 0.0 copy-done
  65.1 0.6 copy.10
Async XLA Ops:
  63.2 1.9 %copy-start = (f32[1,512]{1,0:T(1,128)S(1)}, f32[1,512]{1,0:T(1,128)}, u32[]{:S(2)}) copy-start(f32[1,512]{1,0:T(1,128)} %get-tuple-element.5) | copy-start | bytes 6148

commit v6 on v5

--- a/solution.py
+++ b/solution.py
@@ -44,7 +44,7 @@
     offs, wins, kern_hbm, block_hbm, count_hbm, ray_hbm, slope_hbm,
     out_ref, data_ref,
     block_ref, count_ref, ray_ref, slope_ref,
-    rays1h, ray_high, low1h, high1h, arrived, held,
+    rays1h, rays1h_t, ray_high, low1h, low1h_t, high1h, arrived, held,
     ids_send, ids_recv, w_send, w_recv, f_send, f_swap, f_recv, s_send, s_recv, s_sum,
     acc, model, vec, raw, upd, srch,
     ids_sem, ids_pair, w_sem, w_pair, f_sem, f_pair, s_pair, kern_pair, kern_send, kern_recv, pair_send, pair_recv, load_sem,
@@ -129,7 +129,7 @@
         left = jnp.concatenate(
             [jnp.where(high == r, rows, 0.0) for r in range(ray_parts)], axis=0
         ).astype(BF16)
-        got = lax.dot_general(left, rays1h[...], (((1,), (1,)), ((), ())), preferred_element_type=F32)
+        got = jnp.dot(left, rays1h_t[...], preferred_element_type=F32)
         return cat([jnp.sum(got[8 * r : 8 * r + 8], axis=0, keepdims=True) for r in range(ray_parts)])
 
     def total_of(partials):
@@ -173,6 +173,11 @@
     low_iota = lax.broadcasted_iota(jnp.int32, (LOW, width), 0).astype(F32)
 
     def build_one_hots():
+        @pl.loop(0, wins)
+        def _(p):
+            here = pl.ds(pl.multiple_of(p * slots, slots), slots)
+            rays1h_t[here, :] = rays1h[:, here].astype(F32).T.astype(BF16)
+
         bytes_in(ids_recv.at[0, pl.ds(1, wins - 1)], ids_sem.at[1])
         swap(ids_recv, ids_pair)
         swapped(ids_recv, ids_pair, 1)
@@ -181,7 +186,9 @@
         def _(g):
             low = pieces_of(ids_recv, g * GROUP, 0)
             high = jnp.broadcast_to(pieces_of(ids_recv, g * GROUP, slots), (16, width))
-            low1h[g] = jnp.where(low_iota == low, 1.0, 0.0).astype(BF16)
+            hot = jnp.where(low_iota == low, 1.0, 0.0)
+            low1h[g] = hot.astype(BF16)
+            low1h_t[g] = hot.T.astype(BF16)
             for h in range(HIGH):
                 high1h[g, h] = jnp.where(high == h, 1.0, 0.0).astype(BF16)
 
@@ -245,10 +252,8 @@
                 mask = jnp.concatenate([high1h[g, h]] * (part // 16), axis=0)
                 rows.append(cat([piece * mask for piece in parts]))
             left = jnp.concatenate(rows, axis=0)
-            low = low1h[g]
-            acc[...] += lax.dot_general(
-                left, cat([low, low]), (((1,), (1,)), ((), ())), preferred_element_type=F32
-            )
+            low = low1h_t[g]
+            acc[...] += jnp.dot(left, jnp.concatenate([low, low], axis=0), preferred_element_type=F32)
 
         norms = w_recv[step, :, :, :, slots : 2 * slots].reshape(total, 1, slots)
         beta = jnp.sqrt(total_of(norms))
@@ -391,8 +396,10 @@
             pltpu.VMEM((wins, slots), jnp.int32),
             pltpu.VMEM((1, rays), F32),
             pltpu.VMEM((ray_low, wins * slots), BF16),
+            pltpu.VMEM((wins * slots, ray_low), BF16),
             pltpu.VMEM((8, wins * slots), jnp.int32),
             pltpu.VMEM((groups, LOW, GROUP * slots), BF16),
+            pltpu.VMEM((groups, GROUP * slots, LOW), BF16),
             pltpu.VMEM((groups, HIGH, 16, GROUP * slots), BF16),
             pltpu.VMEM((wins, cells, slots), F32),
             pltpu.VMEM((total, part, slots), F32),

time: 65.9 us -> 65.2 us (0.989)
  Pallas kernels: 62.6 us -> 61.9 us
    pallas_call x1, Pallas kernels: 62.6 us -> 61.9 us  [body(): pl.pallas_call(functools.partial(kernel, offs, wins), out_shape=(jax.Shap...]
where the time goes in v6:
time: 65.2 us; the launch traced here: 65 us
  Pallas kernels  61.9 us (95%)
  local copies, waits for them, and re-layouts  2.45 us (4%)
    pallas_call x1, Pallas kernels, body(): pl.pallas_call(functools.partial(kernel, offs, wins), out_shape=(jax.Shap...  61.9 us
    unnamed x4, local copies, waits for them, and re-layouts  2.45 us

profile of v6, /device:TPU:0, one launch (start us, length us, event | category | flops | bytes accessed | tf_op | source)
XLA Modules:
  0.0 65.0 jit_solution(11956887748762422105)
XLA Ops:
  0.6 61.9 %shard_map.68 = (f32[64,2048]{1,0:T(8,128)}, f32[1,512]{1,0:T(1,128)}) custom-call(f32[1,1,16,64,128]{4,3,2,1,0:T(8,128)} %kern_hbm.1, s32[1,1,16,128]{3,2,1,0:T(8,128)} %block_hbm.1, s32[1,1,16]{2,1,0:T(1,128)} %count_hbm.1, s32[1,1,16,128]{3,2,1,0:T(8,128)} %ray_hbm.1, f32[1,1,512]{2,1,0:T(1,128)} %slope_hbm.1), custom_call_target="tpu_custom_call" | custom-call | tf_op jit(solution)/shard_map/pallas_call | solution.py:385
  62.5 0.0 copy-start
  62.5 1.9 %copy.9 = f32[64,2048]{1,0:T(8,128)} copy(f32[64,2048]{1,0:T(8,128)} %get-tuple-element.8) | data formatting | bytes 1048576
  64.4 0.0 copy-done
  64.4 0.6 copy.10
Async XLA Ops:
  62.5 1.9 %copy-start = (f32[1,512]{1,0:T(1,128)S(1)}, f32[1,512]{1,0:T(1,128)}, u32[]{:S(2)}) copy-start(f32[1,512]{1,0:T(1,128)} %get-tuple-element.5) | copy-start | bytes 6148

commit v7 on v6

--- a/solution.py
+++ b/solution.py
@@ -42,7 +42,7 @@
 
 def kernel(
     offs, wins, kern_hbm, block_hbm, count_hbm, ray_hbm, slope_hbm,
-    out_ref, data_ref,
+    out_upd, out_srch, coef_ref, data_ref,
     block_ref, count_ref, ray_ref, slope_ref,
     rays1h, rays1h_t, ray_high, low1h, low1h_t, high1h, arrived, held,
     ids_send, ids_recv, w_send, w_recv, f_send, f_swap, f_recv, s_send, s_recv, s_sum,
@@ -135,6 +135,15 @@
     def total_of(partials):
         return jnp.sum(jnp.sum(partials, axis=0), axis=1, keepdims=True)
 
+    def write_weights(step, data):
+        weights = take(data)
+        partial = fold(data * data)
+        for p in range(wins):
+            w_send[step, p, :, 0:slots] = weights[:, p * slots : (p + 1) * slots]
+            w_send[step, p, :, slots : 2 * slots] = partial
+
+    write_weights(0, slope_ref[...])
+
     def bytes_in(ref, sem):
         pltpu.make_async_copy(ref, ref, sem).wait()
 
@@ -145,8 +154,8 @@
         ids_send[p, :, slots : 2 * slots] = high.astype(F32)
     ids_recv[0, 0] = ids_send[my_win]
     vec[...] = jnp.zeros_like(vec)
-    srch[my_off] = jnp.zeros_like(vec)
-    upd[my_off] = jnp.zeros_like(vec)
+    srch[...] = jnp.zeros_like(vec)
+    upd[...] = jnp.zeros_like(vec)
     raw[...] = jnp.zeros_like(raw)
 
     pl.semaphore_wait(barrier, wins - 1 + offs - 1)
@@ -195,11 +204,6 @@
     def one_step(step, carry):
         data, alpha, rho, rhobar, phibar, sine, cosine = carry
         first = step == 0
-        weights = take(data)
-        partial = fold(data * data)
-        for p in range(wins):
-            w_send[step, p, :, 0:slots] = weights[:, p * slots : (p + 1) * slots]
-            w_send[step, p, :, slots : 2 * slots] = partial
         to_owner(lambda win: w_send.at[step, win], w_recv.at[step], w_sem.at[0, step], w_sem.at[1, step])
 
         @pl.when(first)
@@ -213,7 +217,7 @@
         for h in range(HIGH):
             fresh = raw[h] / alpha
             vec[h] = fresh
-            srch[my_off, h] = fresh - theta_rho * srch[my_off, h]
+            srch[h] = fresh - theta_rho * srch[h]
         acc[...] = jnp.zeros_like(acc)
 
         w_recv[step, 0, 0] = w_send[step, my_win]
@@ -271,7 +275,7 @@
             square += piece * piece
             for c, half_piece in enumerate(split2(piece)):
                 model[h * part : (h + 1) * part, c * LOW : (c + 1) * LOW] = half_piece
-            upd[my_off, h] = upd[my_off, h] + phi / rho * srch[my_off, h]
+            upd[h] = upd[h] + phi / rho * srch[h]
         norm = fold(jnp.sum(square, axis=0, keepdims=True))
 
         @pl.loop(0, groups)
@@ -313,6 +317,7 @@
         alpha = jnp.sqrt(total_of(f_recv[step, :, :, slots : 2 * slots]))
         terms = cat([f_recv[step, p, :, 0:slots] for p in range(wins)])
         data = gather_rays(terms) / alpha - alpha * data
+        pl.when(step < ITERS - 1)(lambda: write_weights(step + 1, data))
         rhobar = jnp.where(first, alpha, -cosine * alpha)
         sine = jnp.where(first, jnp.zeros_like(sine), sine)
         return data, alpha, rho, rhobar, phibar, sine, cosine
@@ -328,14 +333,18 @@
     to_owner(lambda win: s_send, s_recv, w_sem.at[0, ITERS], w_sem.at[1, ITERS])
     theta_rho = sine * alpha / rho
     for h in range(HIGH):
-        srch[my_off, h] = raw[h] / alpha - theta_rho * srch[my_off, h]
-    for other in range(1, offs):
-        for which, ref in enumerate((upd, srch)):
-            pltpu.make_async_remote_copy(
-                src_ref=ref.at[my_off], dst_ref=ref.at[my_off],
-                send_sem=pair_send.at[which, other], recv_sem=pair_recv.at[which, other],
-                device_id=(off_to[other], my_win), device_id_type=MESH,
-            ).start()
+        srch[h] = raw[h] / alpha - theta_rho * srch[h]
+    outs = ((upd, out_upd), (srch, out_srch))
+
+    @pl.loop(0, HIGH)
+    def _(h):
+        for which, (ref, out) in enumerate(outs):
+            spot = out.at[half(my_off), pl.ds(pl.multiple_of(h * LOW, LOW), LOW)]
+            each_core(lambda c, to, _: remote(
+                ref.at[h], spot, pair_send.at[which, c], pair_recv.at[which, c], to, my_win
+            ))
+            pltpu.make_async_copy(ref.at[h], spot, load_sem.at[which]).start()
+
     bytes_in(s_recv.at[0, pl.ds(1, wins - 1)], w_sem.at[1, ITERS])
     s_sum[0] = jnp.sum(s_recv[0], axis=0)
     swap(s_sum, s_pair)
@@ -344,14 +353,11 @@
     data_ref[...] = data / beta
     rho = jnp.sqrt(rhobar * rhobar + beta * beta)
     phi = rhobar / rho * phibar
-    for other in range(1, offs):
-        for which, ref in enumerate((upd, srch)):
-            bytes_in(ref.at[0], pair_recv.at[which, other])
-    for o in range(offs):
-        for h in range(HIGH):
-            out_ref[o * part : (o + 1) * part, h * LOW : (h + 1) * LOW] = (
-                upd[o, h] + phi / rho * srch[o, h]
-            )
+    coef_ref[...] = jnp.broadcast_to(phi / rho, coef_ref.shape)
+    for which, (_, out) in enumerate(outs):
+        bytes_in(out.at[pl.ds(0, part)], load_sem.at[which])
+        for c in range(1, offs):
+            bytes_in(out.at[pl.ds(0, part)], pair_recv.at[which, c])
 
     others = pl.ds(1, wins - 1)
     bytes_in(ids_recv.at[0, others], ids_sem.at[0])
@@ -367,9 +373,9 @@
             bytes_in(f_swap.at[step, c], f_pair.at[0, step, c])
     bytes_in(s_recv.at[0, others], w_sem.at[0, ITERS])
     swapped(s_sum, s_pair, 0)
-    for other in range(1, offs):
-        for which, ref in enumerate((upd, srch)):
-            bytes_in(ref.at[0], pair_send.at[which, other])
+    for which, (_, out) in enumerate(outs):
+        for c in range(1, offs):
+            bytes_in(out.at[pl.ds(0, part)], pair_send.at[which, c])
 
 
 def body(kernels, blocks, counts, ray_of, slopes):
@@ -381,15 +387,18 @@
     groups = total // GROUP
     ray_low = LOW if rays % LOW == 0 else rays
     vmem = pl.BlockSpec(memory_space=pltpu.VMEM)
+    hbm = pl.BlockSpec(memory_space=pltpu.HBM)
     model = (HIGH, part, LOW)
-    update, data = pl.pallas_call(
+    update, search, coef, data = pl.pallas_call(
         functools.partial(kernel, offs, wins),
         out_shape=(
             jax.ShapeDtypeStruct((cells, BLK_DEV), F32),
+            jax.ShapeDtypeStruct((cells, BLK_DEV), F32),
+            jax.ShapeDtypeStruct((1, LANES), F32),
             jax.ShapeDtypeStruct((1, rays), F32),
         ),
-        in_specs=[pl.BlockSpec(memory_space=pltpu.HBM)] * 5,
-        out_specs=(vmem, vmem),
+        in_specs=[hbm] * 5,
+        out_specs=(hbm, hbm, vmem, vmem),
         scratch_shapes=[
             pltpu.VMEM((wins, slots), jnp.int32),
             pltpu.SMEM((wins,), jnp.int32),
@@ -417,8 +426,8 @@
             pltpu.VMEM((HIGH * part, 2 * LOW), BF16),
             pltpu.VMEM(model, F32),
             pltpu.VMEM(model, F32),
-            pltpu.VMEM((offs,) + model, F32),
-            pltpu.VMEM((offs,) + model, F32),
+            pltpu.VMEM(model, F32),
+            pltpu.VMEM(model, F32),
             pltpu.SemaphoreType.DMA((2,)),
             pltpu.SemaphoreType.DMA((2, offs)),
             pltpu.SemaphoreType.DMA((2, ITERS + 1)),
@@ -437,7 +446,7 @@
             collective_id=0, has_side_effects=True, vmem_limit_bytes=60 * 1024 * 1024
         ),
     )(kernels, blocks, counts, ray_of, slopes)
-    return update, data[None]
+    return update + coef[0, 0] * search, data[None]
 
 
 def solution(mesh):

time: 65.2 us -> 65.5 us (level)
  other arithmetic: 0 us -> 2.08 us
  local copies, waits for them, and re-layouts: 2.45 us -> 1.15 us
    add x0 -> x1, other arithmetic: none -> 2.08 us  [body(): return (update + coef[0, 0] * search, data[None])]
    unnamed x4 -> x5, local copies, waits for them, and re-layouts: 2.45 us -> 1.15 us
where the time goes in v7:
time: 65.5 us; the launch traced here: 65.3 us
  Pallas kernels  61.4 us (94%)
  other arithmetic  2.08 us (3%)
  local copies, waits for them, and re-layouts  1.15 us (2%)
    pallas_call x1, Pallas kernels, body(): pl.pallas_call(functools.partial(kernel, offs, wins), out_shape=(jax.Shap...  61.4 us
    add x1, other arithmetic, body(): return (update + coef[0, 0] * search, data[None])  2.08 us

profile of v7, /device:TPU:0, one launch (start us, length us, event | category | flops | bytes accessed | tf_op | source)
XLA Modules:
  0.0 65.3 jit_solution(11936521443090742341)
XLA Ops:
  0.6 61.4 %shard_map.68 = (f32[64,2048]{1,0:T(8,128)}, f32[64,2048]{1,0:T(8,128)}, f32[1,128]{1,0:T(1,128)}, f32[1,512]{1,0:T(1,128)}) custom-call(f32[1,1,16,64,128]{4,3,2,1,0:T(8,128)} %kern_hbm.1, s32[1,1,16,128]{3,2,1,0:T(8,128)} %block_hbm.1, s32[1,1,16]{2,1,0:T(1,128)} %count_hbm.1, s32[1,1,16,128]{3,2,1,0:T(8,128)} %ray_hbm.1, f32[1,1,512]{2,1,0:T(1,128)} %slope_hbm.1), custom_call_target="tpu_custom_call" | custom-call | tf_op jit(solution)/shard_map/pallas_call | solution.py:392
  62.0 0.0 copy-start.1
  62.0 0.6 copy-done.1
  62.6 0.0 copy-start
  62.6 2.1 %multiply_add_fusion = f32[64,2048]{1,0:T(8,128)} fusion(f32[64,2048]{1,0:T(8,128)} %get-tuple-element.6, f32[64,2048]{1,0:T(8,128)} %get-tuple-element.8, f32[]{:T(128)S(1)} %bitcast.4), kind=kLoop, calls=%fused_computation | loop fusion | flops 262144 | bytes 1572868 | tf_op jit(solution)/shard_map/add | solution.py:449
  64.7 0.0 copy-done
  64.7 0.6 copy.8
Async XLA Ops:
  62.0 0.6 copy-start.1
  62.6 2.1 %copy-start = (f32[1,512]{1,0:T(1,128)S(1)}, f32[1,512]{1,0:T(1,128)}, u32[]{:S(2)}) copy-start(f32[1,512]{1,0:T(1,128)} %get-tuple-element.9) | copy-start | bytes 6148

commit v8 on v6

--- a/solution.py
+++ b/solution.py
@@ -370,6 +370,11 @@
     for other in range(1, offs):
         for which, ref in enumerate((upd, srch)):
             bytes_in(ref.at[0], pair_send.at[which, other])
+
+
+def hand_on(update_ref, data_ref, update_out, data_out):
+    update_out[...] = update_ref[...]
+    data_out[0] = data_ref[...]
 
 
 def body(kernels, blocks, counts, ray_of, slopes):
@@ -437,7 +442,16 @@
             collective_id=0, has_side_effects=True, vmem_limit_bytes=60 * 1024 * 1024
         ),
     )(kernels, blocks, counts, ray_of, slopes)
-    return update, data[None]
+    return pl.pallas_call(
+        hand_on,
+        out_shape=(
+            jax.ShapeDtypeStruct((cells, BLK_DEV), F32),
+            jax.ShapeDtypeStruct((1, 1, rays), F32),
+        ),
+        in_specs=[vmem, vmem],
+        out_specs=(vmem, vmem),
+        compiler_params=pltpu.CompilerParams(vmem_limit_bytes=60 * 1024 * 1024),
+    )(update, data)
 
 
 def solution(mesh):

time: 65.2 us -> 64.6 us (level)
  local copies, waits for them, and re-layouts: 2.45 us -> 0 us
  Pallas kernels: 61.9 us -> 63.8 us
    unnamed x4 -> x0, local copies, waits for them, and re-layouts: 2.45 us -> none
    pallas_call x0 -> x1, Pallas kernels: none -> 1.87 us  [body(): pl.pallas_call(hand_on, out_shape=(jax.ShapeDtypeStruct((cells, BLK_DEV),...]
where the time goes in v8:
time: 64.6 us; the launch traced here: 64.4 us
  Pallas kernels  63.8 us (99%)
    pallas_call x1, Pallas kernels, body(): pl.pallas_call(functools.partial(kernel, offs, wins), out_shape=(jax.Shap...  61.9 us
    pallas_call x1, Pallas kernels, body(): pl.pallas_call(hand_on, out_shape=(jax.ShapeDtypeStruct((cells, BLK_DEV),...  1.87 us

profile of v8, /device:TPU:0, one launch (start us, length us, event | category | flops | bytes accessed | tf_op | source)
XLA Modules:
  0.0 64.4 jit_solution(340802264580854004)
XLA Ops:
  0.6 61.9 %shard_map.68 = (f32[64,2048]{1,0:T(8,128)}, f32[1,512]{1,0:T(1,128)}) custom-call(f32[1,1,16,64,128]{4,3,2,1,0:T(8,128)} %kern_hbm.1, s32[1,1,16,128]{3,2,1,0:T(8,128)} %block_hbm.1, s32[1,1,16]{2,1,0:T(1,128)} %count_hbm.1, s32[1,1,16,128]{3,2,1,0:T(8,128)} %ray_hbm.1, f32[1,1,512]{2,1,0:T(1,128)} %slope_hbm.1), custom_call_target="tpu_custom_call" | custom-call | tf_op jit(solution)/shard_map/pallas_call | solution.py:390
  62.5 1.9 %shard_map.69 = (f32[64,2048]{1,0:T(8,128)}, f32[1,1,512]{2,1,0:T(1,128)}) custom-call(f32[64,2048]{1,0:T(8,128)} %get-tuple-element.4.update_ref, f32[1,512]{1,0:T(1,128)} %get-tuple-element.5.data_ref), custom_call_target="tpu_custom_call" | custom-call | tf_op jit(solution)/shard_map/pallas_call | solution.py:445
